TPU v7x, 32 devices: a whole 2x2x4 slice. The times are simulated.
32 devices in a mesh: tile: 8 (over z, y), spec: 4 (over x, core).
Axes of the slice: x: 2, y: 2, z: 4, core: 2. Of those that a mesh axis runs over, the one named last changes fastest.
Arguments:
- latent: bfloat16 [32, 2048, 1024], P(None, ('tile', 'spec')), may hold values from -6 to 6
- basis: bfloat16 [224, 32], replicated, may hold values from -1 to 1
- response: bfloat16 [8, 224], replicated, may hold values from -0.375 to 0.375
- hyper_obs: bfloat16 [224, 512, 256], P('spec', 'tile'), may hold values from -6 to 6
- multi_obs: bfloat16 [8, 2048, 1024], P(None, ('tile', 'spec')), may hold values from -6 to 6
Outputs:
- z_next: bfloat16 [32, 2048, 1024], P(None, ('tile', 'spec'))
- hs_residual: bfloat16 [224, 512, 256], P('spec', 'tile')
All inputs are finite; a program needn't handle non-finite values.
Results may differ from a plain program's by a relative error of at most 0.0054.
Values may be sent and summed in bfloat16 or wider, within the bound.
A program may use at most 128 MiB of HBM per device.

v0:
```python
import jax
import jax.numpy as jnp
from jax import lax
from jax.sharding import PartitionSpec as P

DECIM = 4
HALO = 128


step_size = 0.3


def with_halo(cells, sides, width):
    for axis, dim in sides:
        count = lax.axis_size(axis)
        ends = count - 1
        head = lax.slice_in_dim(cells, 0, width, axis=dim)
        tail = lax.slice_in_dim(cells, cells.shape[dim] - width, cells.shape[dim], axis=dim)
        cells = jnp.concatenate(
            [
                lax.ppermute(tail, axis, [(i, (i + 1) % count) for i in range(ends)]),
                cells,
                lax.ppermute(head, axis, [((i + 1) % count, i) for i in range(ends)]),
            ],
            axis=dim,
        )
    return cells


def profile(where_at):
    narrow = DECIM / 2.0
    decay_len = 3.0 * HALO / 8.0
    ripple = jnp.cos(where_at * (jnp.pi / 7.0))
    return (
        jnp.exp(-where_at * where_at / (2.0 * narrow * narrow))
        + 0.5 * jnp.exp(-jnp.abs(where_at) / decay_len) * ripple * ripple
    )


def kernel_values(offsets):
    every_offset = jnp.arange(-HALO, HALO + 1).astype(jnp.float32)
    energy = jnp.sqrt(jnp.sum(profile(every_offset) ** 2))
    inside = jnp.abs(offsets) <= HALO
    return jnp.where(inside, profile(offsets.astype(jnp.float32)) / energy, 0.0).astype(
        jnp.bfloat16
    )


def column_matrix(fine_count, coarse_count):
    fine_cols = jnp.arange(fine_count)[:, None]
    coarse = jnp.arange(coarse_count)[None, :]
    return kernel_values(fine_cols - DECIM * coarse)


def row_matrix(rows_local):
    coarse = jnp.arange(rows_local // DECIM)[:, None]
    padded = jnp.arange(rows_local + 2 * HALO)[None, :]
    return kernel_values(padded - HALO - DECIM * coarse)


def back_matrix(rows_local):
    fine_rows = jnp.arange(rows_local)[:, None]
    coarse = jnp.arange(rows_local // DECIM + 2 * (HALO // DECIM))[None, :]
    return kernel_values(fine_rows - DECIM * coarse + HALO)


def shards(latent, basis, response, hyper_obs, multi_obs):
    highest = lax.Precision.HIGHEST
    rows_dev = hyper_obs.shape[1] * DECIM
    width_cols = latent.shape[2]
    spectra = jnp.einsum("bk,krc->brc", basis, latent, preferred_element_type=jnp.float32).astype(
        jnp.bfloat16
    )
    column_kernel = column_matrix(width_cols, width_cols // DECIM)
    column_wide = column_kernel.astype(jnp.float32)
    narrow_pixel = jnp.einsum(
        "brc,cj->brj", spectra, column_kernel, preferred_element_type=jnp.float32
    )
    narrow_band = lax.all_to_all(narrow_pixel, "spec", split_axis=0, concat_axis=1, tiled=True)
    padded = with_halo(narrow_band, (("tile", 1),), HALO)
    row_kernel = row_matrix(rows_dev).astype(jnp.float32)
    blurred = jnp.einsum("ir,brj->bij", row_kernel, padded, precision=highest)
    hs_residual = (blurred - hyper_obs.astype(jnp.float32)).astype(jnp.bfloat16)
    coarse_padded = with_halo(hs_residual, (("tile", 1),), HALO // DECIM)
    rows_back = jnp.einsum(
        "rq,bqj->brj", back_matrix(rows_dev), coarse_padded, preferred_element_type=jnp.float32
    )
    multi_resid = (
        jnp.einsum("mb,brc->mrc", response, spectra, preferred_element_type=jnp.float32)
        - multi_obs.astype(jnp.float32)
    ).astype(jnp.bfloat16)
    rows_pixel = lax.all_to_all(rows_back, "spec", split_axis=1, concat_axis=0, tiled=True)
    spread_pixel = jnp.einsum("brj,cj->brc", rows_pixel, column_wide, precision=highest).astype(
        jnp.bfloat16
    )
    spread_wide = lax.optimization_barrier(spread_pixel).astype(jnp.float32)
    multi_back = jnp.einsum(
        "mb,mrc->brc", response, multi_resid, preferred_element_type=jnp.float32
    )
    spectral = (spread_wide + multi_back).astype(jnp.bfloat16)
    gradient = jnp.einsum("bk,brc->krc", basis, spectral, preferred_element_type=jnp.float32)
    z_next = (latent.astype(jnp.float32) - step_size * gradient).astype(jnp.bfloat16)
    return (z_next, hs_residual)


def solution(mesh):
    in_specs = (
        P(None, ("tile", "spec"), None),
        P(),
        P(),
        P("spec", "tile", None),
        P(None, ("tile", "spec"), None),
    )
    out_specs = (P(None, ("tile", "spec"), None), P("spec", "tile", None))
    return jax.shard_map(shards, mesh=mesh, in_specs=in_specs, out_specs=out_specs, check_vma=False)
```

profile of v0, /device:TPU:8, one launch (start us, length us, event | category | flops | bytes accessed | tf_op | source)
XLA Modules:
  0.0 912.3 jit_solution(1004611074523642593)
XLA Ops:
  2.0 14.7 %convolution_convert_fusion.1 = bf16[224,64,1024]{2,0,1:T(8,128)(2,1)} fusion(bf16[32,64,1024]{2,1,0:T(8,128)(2,1)} %param.5, bf16[224,32]{0,1:T(8,128)(2,1)S(1)} %copy-done), kind=kOutput, calls=%fused_computation.13 | convolution fusion | flops 954204160 | bytes 33568768 | tf_op jit(solution)/shard_map/bk,krc->brc/dot_general | solution.py:71
  16.7 44.0 %fusion.9 = f32[224,64,256]{2,1,0:T(8,128)} fusion(bf16[224,64,1024]{2,0,1:T(8,128)(2,1)} %convolution_convert_fusion.1, f32[]{:T(128)S(6)} %sqrt.2, s32[256]{0:T(256)S(1)} %iota_multiply_fusion), kind=kOutput, calls=%fused_computation.9 | convolution fusion | flops 7520911360 | bytes 44041220 | tf_op jit(solution)/shard_map/brc,cj->brj/dot_general | solution.py:76
  60.7 170.8 %all_to_all.36 = f32[224,64,256]{2,1,0:T(8,128)} all-to-all(f32[224,64,256]{2,1,0:T(8,128)} %fusion.9), channel_id=1, replica_groups=mesh['tile'=8,'spec'=4] {'spec'}, dimensions={0} | all-to-all | bytes 29360128 | tf_op jit(solution)/shard_map/all_to_all | solution.py:79
  231.5 13.1 %copy.24 = f32[56,4,64,256]{3,2,1,0:T(8,128)} copy(f32[56,4,64,256]{3,2,0,1:T(8,128)} %bitcast.59) | data formatting | bytes 29360128 | tf_op jit(solution)/shard_map/all_to_all | solution.py:79
  244.6 12.1 %fusion.119 = (f32[56,128,256]{2,1,0:T(8,128)}, f32[56,128,256]{2,1,0:T(8,128)}) fusion(f32[56,256,256]{2,1,0:T(8,128)} %bitcast.57), kind=kLoop, calls=%fused_computation.131 | loop fusion | bytes 29360128 | tf_op jit(solution)/shard_map/slice | solution.py:18
  256.8 3.4 collective-permute-start
  260.2 3.3 collective-permute-start.1
  263.5 311.1 %collective-permute-done = f32[56,128,256]{2,1,0:T(8,128)S(1)} collective-permute-done((f32[56,128,256]{2,1,0:T(8,128)}, f32[56,128,256]{2,1,0:T(8,128)S(1)}, u32[]{:S(2)}, u32[]{:S(2)}) %collective-permute-start) | collective-permute-done | bytes 7340064 | tf_op jit(solution)/shard_map/ppermute | solution.py:21
  574.6 3.0 copy-done.4
  577.6 18.0 %fusion.21 = bf16[56,64,256]{2,1,0:T(8,128)(2,1)S(1)} fusion(bf16[56,64,256]{2,1,0:T(8,128)(2,1)} %param.8, f32[56,128,256]{2,1,0:T(8,128)} %collective-permute-done.1, f32[56,256,256]{2,1,0:T(8,128)} %bitcast.58, f32[56,128,256]{2,1,0:T(8,128)} %copy-done.4, f32[]{:T(128)S(6)} %sqrt.2, s32[64]{0:T(128)S(1)} %iota_multiply_fusion.2, s32[512]{0:T(512)S(1)} %iota_add_fusion), kind=kOutput, calls=%fused_computation.25 | convolution fusion | flops 5655166976 | bytes 33032452 | tf_op jit(solution)/shard_map/ir,brj->bij/dot_general | solution.py:82
  595.8 4.3 collective-permute-start.2
  600.1 2.5 collective-permute-start.3
  602.6 35.5 %collective-permute-done.2 = bf16[56,32,256]{2,1,0:T(8,128)(2,1)S(1)} collective-permute-done((bf16[56,32,256]{2,1,0:T(8,128)(2,1)S(1)}, bf16[56,32,256]{2,1,0:T(8,128)(2,1)S(1)}, u32[]{:S(2)}, u32[]{:S(2)}) %collective-permute-start.2) | collective-permute-done | bytes 917536 | tf_op jit(solution)/shard_map/ppermute | solution.py:21
  638.0 1.4 collective-permute-done.3
  639.4 6.8 convolution_bitcast_fusion
  646.2 15.7 %copy.26 = f32[56,256,256]{2,0,1:T(8,128)} copy(f32[56,256,256]{1,2,0:T(8,128)} %convolution_bitcast_fusion) | data formatting | bytes 29360128 | tf_op jit(solution)/shard_map/rq,bqj->brj/transpose | solution.py:85
  661.9 6.8 all-to-all-start.1
  668.7 4.4 fusion.126
  673.1 17.1 %fusion.24 = bf16[8,64,1024]{2,0,1:T(8,128)(2,1)S(1)} fusion(bf16[224,64,1024]{2,0,1:T(8,128)(2,1)} %convolution_convert_fusion.1, bf16[8,64,1024]{2,1,0:T(8,128)(2,1)S(1)} %copy-done.2, bf16[8,224]{1,0:T(8,128)(2,1)S(1)} %copy-done.3), kind=kOutput, calls=%fused_computation.27 | convolution fusion | flops 236453888 | bytes 31460864 | tf_op jit(solution)/shard_map/mb,brc->mrc/dot_general | solution.py:89
  690.3 139.0 %all-to-all-done.1 = f32[56,256,256]{2,0,1:T(8,128)} async-done(((f32[56,256,256]{2,0,1:T(8,128)}), f32[56,256,256]{2,0,1:T(8,128)}, u32[]{:S(2)}, u32[]{:S(2)}) %all-to-all-start.1) | async-done | bytes 14680096 | tf_op jit(solution)/shard_map/all_to_all | solution.py:92
  829.3 14.9 %copy.28 = f32[4,56,64,256]{3,2,1,0:T(8,128)} copy(f32[4,56,64,256]{3,1,2,0:T(8,128)} %bitcast.11) | data formatting | bytes 29360128 | tf_op jit(solution)/shard_map/all_to_all | solution.py:92
  844.3 37.2 %convolution_convert_fusion = bf16[224,64,1024]{2,0,1:T(8,128)(2,1)} fusion(f32[224,64,256]{2,1,0:T(8,128)} %bitcast.56, bf16[1024,256,1]{1,0,2:T(8,128)(2,1)S(1)} %fusion.126), kind=kOutput, calls=%fused_computation.12 | convolution fusion | flops 45111836672 | bytes 44564480 | tf_op jit(solution)/shard_map/brj,cj->brc/dot_general | solution.py:93
  881.4 24.0 %fusion.14 = bf16[32,64,1024]{2,0,1:T(8,128)(2,1)} fusion(bf16[32,64,1024]{2,1,0:T(8,128)(2,1)} %param.5, bf16[224,64,1024]{2,0,1:T(8,128)(2,1)} %convolution_convert_fusion, bf16[8,64,1024]{2,0,1:T(8,128)(2,1)S(1)} %fusion.24, bf16[224,32]{0,1:T(8,128)(2,1)S(1)} %copy-done, bf16[8,224]{1,0:T(8,128)(2,1)S(1)} %copy-done.3), kind=kOutput, calls=%fused_computation.17 | convolution fusion | flops 1226833920 | bytes 38815232 | tf_op jit(solution)/shard_map/bk,brc->krc/dot_general | solution.py:101
  905.5 6.5 copy.31
  (16 shorter events, 0.9 us)
Async XLA Ops:
  0.6 1.4 copy-start
  256.8 317.9 %collective-permute-start = (f32[56,128,256]{2,1,0:T(8,128)}, f32[56,128,256]{2,1,0:T(8,128)S(1)}, u32[]{:S(2)}, u32[]{:S(2)}) collective-permute-start(f32[56,128,256]{2,1,0:T(8,128)} %get-tuple-element.8), channel_id=1, source_target_pairs={{0,4},{4,8},{8,12},{12,16},{16,20},{20,24},{24,28},{1,5},{5,9},{9,... | collective-permute-start | bytes 22020104 | tf_op jit(solution)/shard_map/ppermute | solution.py:21
  260.2 317.4 %collective-permute-start.1 = (f32[56,128,256]{2,1,0:T(8,128)}, f32[56,128,256]{2,1,0:T(8,128)}, u32[]{:S(2)}, u32[]{:S(2)}) collective-permute-start(f32[56,128,256]{2,1,0:T(8,128)} %get-tuple-element.9), channel_id=1, source_target_pairs={{4,0},{8,4},{12,8},{16,12},{20,16},{24,20},{28,24},{5,1},{9,5},{13... | collective-permute-start | bytes 22020104 | tf_op jit(solution)/shard_map/ppermute | solution.py:23
  574.6 3.0 copy-start.4
  595.6 50.6 %copy-start.1 = (bf16[56,64,256]{2,1,0:T(8,128)(2,1)}, bf16[56,64,256]{2,1,0:T(8,128)(2,1)S(1)}, u32[]{:S(2)}) copy-start(bf16[56,64,256]{2,1,0:T(8,128)(2,1)S(1)} %fusion.21) | copy-start | bytes 5505028
  595.8 42.3 %collective-permute-start.2 = (bf16[56,32,256]{2,1,0:T(8,128)(2,1)S(1)}, bf16[56,32,256]{2,1,0:T(8,128)(2,1)S(1)}, u32[]{:S(2)}, u32[]{:S(2)}) collective-permute-start(bf16[56,32,256]{2,1,0:T(8,128)(2,1)S(1)} %get-tuple-element.10), channel_id=1, source_target_pairs={{0,4},{4,8},{8,12},{12,16},{16,20},{20,24},{24,28},{1,5},{5,9},{9,... | collective-permute-start | bytes 2752520 | tf_op jit(solution)/shard_map/ppermute | solution.py:21
  600.1 39.3 %collective-permute-start.3 = (bf16[56,32,256]{2,1,0:T(8,128)(2,1)S(1)}, bf16[56,32,256]{2,1,0:T(8,128)(2,1)S(1)}, u32[]{:S(2)}, u32[]{:S(2)}) collective-permute-start(bf16[56,32,256]{2,1,0:T(8,128)(2,1)S(1)} %get-tuple-element.11), channel_id=1, source_target_pairs={{4,0},{8,4},{12,8},{16,12},{20,16},{24,20},{28,24},{5,1},{9,5},{13... | collective-permute-start | bytes 2752520 | tf_op jit(solution)/shard_map/ppermute | solution.py:23
  661.9 11.2 %copy-start.2 = (bf16[8,64,1024]{2,1,0:T(8,128)(2,1)S(1)}, bf16[8,64,1024]{2,1,0:T(8,128)(2,1)}, u32[]{:S(2)}) copy-start(bf16[8,64,1024]{2,1,0:T(8,128)(2,1)} %param.9) | copy-start | bytes 3145732
  661.9 11.2 %copy-start.3 = (bf16[8,224]{1,0:T(8,128)(2,1)S(1)}, bf16[8,224]{1,0:T(8,128)(2,1)}, u32[]{:S(2)}) copy-start(bf16[8,224]{1,0:T(8,128)(2,1)} %param.7) | copy-start | bytes 10756
  661.9 167.4 %all-to-all-start.1 = ((f32[56,256,256]{2,0,1:T(8,128)}), f32[56,256,256]{2,0,1:T(8,128)}, u32[]{:S(2)}, u32[]{:S(2)}) async-start(f32[56,256,256]{2,0,1:T(8,128)} %copy.26), calls=%async_computation.1 | async-start | bytes 29360128 | tf_op jit(solution)/shard_map/all_to_all | solution.py:92
where the time goes:
time: 916 us; the launch traced here: 912 us
  waiting for transfers between devices  487 us (53%)
  blocking collectives  171 us (19%)
  matrix products  162 us (18%)
  local copies, waits for them, and re-layouts  65.6 us (7%)
  starting transfers between devices  20.2 us (2%)
    ppermute x2, waiting for transfers between devices, with_halo(): lax.ppermute(tail, axis, [(i, (i + 1) % count) for i in range(ends)])  347 us
    all_to_all x1, blocking collectives, shards(): lax.all_to_all(narrow_pixel, 'spec', split_axis=0, concat_axis=1, tiled=T...  171 us
    all_to_all x1, waiting for transfers between devices, shards(): lax.all_to_all(rows_back, 'spec', split_axis=1, concat_axis=0, tiled=True)  139 us
    dot_general x1, matrix products, shards(): jnp.einsum('brc,cj->brj', spectra, column_kernel, preferred_element_type=...  44 us
    dot_general x1, matrix products, shards(): jnp.einsum('brj,cj->brc', rows_pixel, column_wide, precision=highest)  37.2 us
    dot_general x1, matrix products, shards(): jnp.einsum('bk,brc->krc', basis, spectral, preferred_element_type=jnp.flo...  24 us
  transfers between devices with their start and end apart: 5, of which 4 were waited for; matrix products, arithmetic and copies ran while one was open for 2% of the time, Pallas kernels for 0%

commit v1 on v0

v1 whole, which is shorter than its diff:
```python
import jax
import jax.numpy as jnp
import numpy as np
from jax import lax
from jax.sharding import PartitionSpec as P

DECIM = 4
HALO = 128
RIM = HALO // DECIM
STEP = 0.3


def profile(where_at):
    narrow = np.float32(DECIM / 2.0)
    decay_len = np.float32(3.0 * HALO / 8.0)
    ripple = np.cos(where_at * np.float32(np.pi / 7.0))
    return np.exp(-where_at * where_at / (np.float32(2.0) * narrow * narrow)) + np.float32(
        0.5
    ) * np.exp(-np.abs(where_at) / decay_len) * ripple * ripple


def kernel_values(offsets):
    every_offset = np.arange(-HALO, HALO + 1).astype(np.float32)
    energy = np.sqrt(np.sum(profile(every_offset) ** 2))
    inside = np.abs(offsets) <= HALO
    return np.where(inside, profile(offsets.astype(np.float32)) / energy, np.float32(0.0)).astype(
        jnp.bfloat16
    )


def column_matrix(fine_count):
    return kernel_values(np.arange(fine_count)[:, None] - DECIM * np.arange(fine_count // DECIM)[None, :])


def dot(spec, a, b):
    return jnp.einsum(spec, a, b, preferred_element_type=jnp.float32)


def shards(latent, basis, response, hyper_obs, multi_obs):
    bf16 = jnp.bfloat16
    f32 = jnp.float32
    group = hyper_obs.shape[0]
    coarse = hyper_obs.shape[1]
    rows_dev = coarse * DECIM
    count = lax.axis_size("tile")
    up = [(i + 1, i) for i in range(count - 1)]
    down = [(i, i + 1) for i in range(count - 1)]
    cols = column_matrix(latent.shape[2])
    rows = kernel_values(
        np.arange(rows_dev)[:, None] - DECIM * (np.arange(coarse + 2 * RIM)[None, :] - RIM)
    )
    cols = jnp.asarray(cols)
    rows = jnp.asarray(rows)

    narrow = dot("qrc,cj->qrj", latent, cols).astype(bf16)
    narrow = lax.all_to_all(narrow, "spec", split_axis=0, concat_axis=1, tiled=True)
    part = dot("ri,qrj->qij", rows, narrow)
    above = lax.ppermute(part[:, :RIM].astype(bf16), "tile", up)
    below = lax.ppermute(part[:, RIM + coarse :].astype(bf16), "tile", down)
    own = part[:, RIM : RIM + coarse]
    zeros = jnp.zeros((own.shape[0], coarse - RIM, own.shape[2]), f32)
    own = (
        own
        + jnp.concatenate([below.astype(f32), zeros], axis=1)
        + jnp.concatenate([zeros, above.astype(f32)], axis=1)
    ).astype(bf16)
    blurred = lax.all_gather(own, "spec", axis=0, tiled=True)
    mine = lax.dynamic_slice_in_dim(basis, lax.axis_index("spec") * group, group, 0)
    hs_residual = (dot("bq,qij->bij", mine, blurred) - hyper_obs.astype(f32)).astype(bf16)
    back = dot("bq,bij->qij", mine, hs_residual).astype(bf16)
    back = lax.all_to_all(back, "spec", split_axis=0, concat_axis=0, tiled=True)
    back = back.reshape((lax.axis_size("spec"), -1) + back.shape[1:])
    back = jnp.sum(back.astype(f32), axis=0).astype(bf16)
    from_below = lax.ppermute(back[:, :RIM], "tile", up)
    from_above = lax.ppermute(back[:, coarse - RIM :], "tile", down)
    padded = jnp.concatenate([from_above, back, from_below], axis=1)
    rows_back = dot("ri,qij->qrj", rows, padded).astype(bf16)
    rows_back = lax.all_to_all(rows_back, "spec", split_axis=1, concat_axis=0, tiled=True)
    spread = dot("qrj,cj->qrc", rows_back, cols)
    mixed = dot("mb,bq->mq", response, basis).astype(bf16)
    multi_resid = (dot("mq,qrc->mrc", mixed, latent) - multi_obs.astype(f32)).astype(bf16)
    gradient = spread + dot("mq,mrc->qrc", mixed, multi_resid)
    z_next = (latent.astype(f32) - STEP * gradient).astype(bf16)
    return (z_next, hs_residual)


def solution(mesh):
    in_specs = (
        P(None, ("tile", "spec"), None),
        P(),
        P(),
        P("spec", "tile", None),
        P(None, ("tile", "spec"), None),
    )
    out_specs = (P(None, ("tile", "spec"), None), P("spec", "tile", None))
    return jax.shard_map(shards, mesh=mesh, in_specs=in_specs, out_specs=out_specs, check_vma=False)
```

time: 916 us -> 145 us (0.16)
  waiting for transfers between devices: 487 us -> 42 us
  blocking collectives: 171 us -> 34 us
  matrix products: 162 us -> 31.6 us
  local copies, waits for them, and re-layouts: 65.6 us -> 4.91 us
  between operations: 1.73 us -> 14.2 us
    ppermute x4, waiting for transfers between devices: 348 us -> 24.4 us  [the longest x1 18.7 us: shards(): from_above = lax.ppermute(back[:, coarse - RIM:], 'tile', down)]
    all_to_all x1, waiting for transfers between devices: 139 us -> 0.88 us  [shards(): lax.all_to_all(rows_back, 'spec', split_axis=1, concat_axis=0, tiled=True)]
    all_to_all x1 -> x2, blocking collectives: 171 us -> 34 us  [the longest x1 17.2 us: shards(): lax.all_to_all(narrow, 'spec', split_axis=0, concat_axis=1, tiled=True)]
    dot_general x7 -> x8, matrix products: 162 us -> 31.6 us  [dot(): return jnp.einsum(spec, a, b, preferred_element_type=jnp.float32)]
    all_gather x0 -> x1, waiting for transfers between devices: none -> 16.7 us  [shards(): blurred = lax.all_gather(own, 'spec', axis=0, tiled=True)]
    transpose x1 -> x0, local copies, waits for them, and re-layouts: 15.7 us -> none  [shards(): jnp.einsum('rq,bqj->brj', back_matrix(rows_dev), coarse_padded, preferred...]
    all_to_all x1, local copies, waits for them, and re-layouts: 14.9 us -> 0.24 us  [shards(): lax.all_to_all(rows_back, 'spec', split_axis=1, concat_axis=0, tiled=True)]
    all_to_all x1, local copies, waits for them, and re-layouts: 13.1 us -> 0.1 us  [shards(): lax.all_to_all(narrow, 'spec', split_axis=0, concat_axis=1, tiled=True)]
  transfers between devices with their start and end apart: 5 -> 6, of which waited for: 4 -> 6; matrix products, arithmetic and copies ran while one was open for 2% -> 9% of each run, Pallas kernels for 0% -> 0%
where the time goes in v1:
time: 145 us
  waiting for transfers between devices  42 us (29%)
  blocking collectives  34 us (23%)
  matrix products  31.6 us (22%)
  starting transfers between devices  17.2 us (12%)
  between operations  14.2 us (10%)
  local copies, waits for them, and re-layouts  4.91 us (3%)
    dot_general x8, matrix products, dot(): return jnp.einsum(spec, a, b, preferred_element_type=jnp.float32)  31.6 us
    ppermute x1, waiting for transfers between devices, shards(): from_above = lax.ppermute(back[:, coarse - RIM:], 'tile', down)  18.7 us
    all_to_all x1, blocking collectives, shards(): lax.all_to_all(narrow, 'spec', split_axis=0, concat_axis=1, tiled=True)  17.2 us
    all_to_all x1, blocking collectives, shards(): back = lax.all_to_all(back, 'spec', split_axis=0, concat_axis=0, tiled=True)  16.9 us
    all_gather x1, waiting for transfers between devices, shards(): blurred = lax.all_gather(own, 'spec', axis=0, tiled=True)  16.7 us
    all_to_all x1, starting transfers between devices, shards(): lax.all_to_all(rows_back, 'spec', split_axis=1, concat_axis=0, tiled=True)  3.7 us
    ppermute x1, starting transfers between devices, shards(): below = lax.ppermute(part[:, RIM + coarse:].astype(bf16), 'tile', down)  3.43 us
    ppermute x1, starting transfers between devices, shards(): from_above = lax.ppermute(back[:, coarse - RIM:], 'tile', down)  3.38 us
  transfers between devices with their start and end apart: 6, of which 6 were waited for; matrix products, arithmetic and copies ran while one was open for 9% of the time, Pallas kernels for 0%

profile of v1, /device:TPU:8, one launch (start us, length us, event | category | flops | bytes accessed | tf_op | source)
XLA Modules:
  0.0 145.0 jit_solution(6413531473428507624)
XLA Ops:
  7.2 3.6 %fusion.8 = bf16[32,64,256]{2,1,0:T(8,128)(2,1)S(1)} fusion(bf16[1024,256,1]{1,0,2:T(8,128)(2,1)} %constant.27, bf16[32,64,1024]{2,1,0:T(8,128)(2,1)} %param.7), kind=kOutput, calls=%fused_computation.12 | convolution fusion | flops 1074266112 | bytes 5767168 | tf_op jit(solution)/shard_map/qrc,cj->qrj/dot_general | solution.py:36
  10.9 17.2 %all_to_all.41 = bf16[32,64,256]{2,1,0:T(8,128)(2,1)S(1)} all-to-all(bf16[32,64,256]{2,1,0:T(8,128)(2,1)S(1)} %fusion.8), channel_id=1, replica_groups=mesh['tile'=8,'spec'=4] {'spec'}, dimensions={0} | all-to-all | bytes 2097152 | tf_op jit(solution)/shard_map/all_to_all | solution.py:56
  28.1 0.3 fusion.31
  28.5 3.4 %collective-permute-start = (bf16[8,32,256]{2,1,0:T(8,128)(2,1)S(1)}, bf16[8,32,256]{2,1,0:T(8,128)(2,1)S(1)}, u32[]{:S(2)}, u32[]{:S(2)}) collective-permute-start(bf16[8,32,256]{2,1,0:T(8,128)(2,1)S(1)} %get-tuple-element.10), channel_id=1, source_target_pairs={{0,4},{4,8},{8,12},{12,16},{16,20},{20,24},{24,28},{1,5},{5,9},{9,... | collective-permute-start | bytes 393224 | tf_op jit(solution)/shard_map/ppermute | solution.py:59
  31.9 3.3 %collective-permute-start.1 = (bf16[8,32,256]{2,1,0:T(8,128)(2,1)S(1)}, bf16[8,32,256]{2,1,0:T(8,128)(2,1)S(1)}, u32[]{:S(2)}, u32[]{:S(2)}) collective-permute-start(bf16[8,32,256]{2,1,0:T(8,128)(2,1)S(1)} %get-tuple-element.11), channel_id=1, source_target_pairs={{4,0},{8,4},{12,8},{16,12},{20,16},{24,20},{28,24},{5,1},{9,5},{13... | collective-permute-start | bytes 393224 | tf_op jit(solution)/shard_map/ppermute | solution.py:58
  35.2 1.1 collective-permute-done
  36.3 2.7 %collective-permute-done.1 = bf16[8,32,256]{2,1,0:T(8,128)(2,1)S(1)} collective-permute-done((bf16[8,32,256]{2,1,0:T(8,128)(2,1)S(1)}, bf16[8,32,256]{2,1,0:T(8,128)(2,1)S(1)}, u32[]{:S(2)}, u32[]{:S(2)}) %collective-permute-start.1) | collective-permute-done | bytes 131104 | tf_op jit(solution)/shard_map/ppermute | solution.py:58
  39.0 0.8 fusion.16
  39.8 16.7 %all-gather.2.cloned.1.call-done = bf16[32,64,256]{2,1,0:T(8,128)(2,1)} async-done(((bf16[8,64,256]{2,1,0:T(8,128)(2,1)}), bf16[32,64,256]{2,1,0:T(8,128)(2,1)}) %all-gather.2.cloned.1.call-update) | async-done | bytes 1048592 | tf_op jit(solution)/shard_map/all_gather | solution.py:67
  56.6 3.8 %subtract_convert_fusion = bf16[56,64,256]{2,0,1:T(8,128)(2,1)S(1)} fusion(bf16[56,64,256]{2,1,0:T(8,128)(2,1)} %param.10, bf16[32,64,256]{2,1,0:T(8,128)(2,1)} %all-gather.2.cloned.1.call-done, bf16[224,32]{0,1:T(8,128)(2,1)S(1)} %copy-done, s32[]{:T(128)S(6)} %select_n.3), kind=kOutput, calls=%fused_computation.6 | convolution fusion | flops 61472768 | bytes 4726788 | tf_op jit(solution)/shard_map/bq,qij->bij/dot_general | solution.py:36
  60.4 0.5 convolution_convert_fusion.1
  60.9 0.6 copy.29
  61.5 16.9 %all_to_all.42 = bf16[32,64,256]{2,1,0:T(8,128)(2,1)S(1)} all-to-all(bf16[32,64,256]{2,1,0:T(8,128)(2,1)S(1)} %copy.29), channel_id=1, replica_groups=mesh['tile'=8,'spec'=4] {'spec'}, dimensions={0} | all-to-all | bytes 2097152 | tf_op jit(solution)/shard_map/all_to_all | solution.py:71
  79.1 3.4 %collective-permute-start.2 = (bf16[8,32,256]{1,2,0:T(8,128)(2,1)S(1)}, bf16[8,32,256]{1,2,0:T(8,128)(2,1)S(1)}, u32[]{:S(2)}, u32[]{:S(2)}) collective-permute-start(bf16[8,32,256]{1,2,0:T(8,128)(2,1)S(1)} %get-tuple-element.8), channel_id=1, source_target_pairs={{0,4},{4,8},{8,12},{12,16},{16,20},{20,24},{24,28},{1,5},{5,9},{9,... | collective-permute-start | bytes 393224 | tf_op jit(solution)/shard_map/ppermute | solution.py:75
  82.5 3.4 %collective-permute-start.3 = (bf16[8,32,256]{1,2,0:T(8,128)(2,1)S(1)}, bf16[8,32,256]{1,2,0:T(8,128)(2,1)S(1)}, u32[]{:S(2)}, u32[]{:S(2)}) collective-permute-start(bf16[8,32,256]{1,2,0:T(8,128)(2,1)S(1)} %get-tuple-element.9), channel_id=1, source_target_pairs={{4,0},{8,4},{12,8},{16,12},{20,16},{24,20},{28,24},{5,1},{9,5},{13... | collective-permute-start | bytes 393224 | tf_op jit(solution)/shard_map/ppermute | solution.py:74
  85.9 18.7 %collective-permute-done.2 = bf16[8,32,256]{1,2,0:T(8,128)(2,1)S(1)} collective-permute-done((bf16[8,32,256]{1,2,0:T(8,128)(2,1)S(1)}, bf16[8,32,256]{1,2,0:T(8,128)(2,1)S(1)}, u32[]{:S(2)}, u32[]{:S(2)}) %collective-permute-start.2) | collective-permute-done | bytes 131104 | tf_op jit(solution)/shard_map/ppermute | solution.py:75
  104.5 1.9 %collective-permute-done.3 = bf16[8,32,256]{1,2,0:T(8,128)(2,1)S(1)} collective-permute-done((bf16[8,32,256]{1,2,0:T(8,128)(2,1)S(1)}, bf16[8,32,256]{1,2,0:T(8,128)(2,1)S(1)}, u32[]{:S(2)}, u32[]{:S(2)}) %collective-permute-start.3) | collective-permute-done | bytes 131104 | tf_op jit(solution)/shard_map/ppermute | solution.py:74
  106.4 0.6 fusion.7
  107.1 1.8 %copy.35 = bf16[8,256,256]{2,0,1:T(8,128)(2,1)} copy(bf16[8,256,256]{1,2,0:T(8,128)(2,1)S(1)} %fusion.7) | data formatting | bytes 2097152 | tf_op jit(solution)/shard_map/convert_element_type | solution.py:77
  108.9 3.7 %all-to-all-start.2 = ((bf16[8,256,256]{2,0,1:T(8,128)(2,1)}), bf16[8,256,256]{2,0,1:T(8,128)(2,1)S(1)}, u32[]{:S(2)}, u32[]{:S(2)}) async-start(bf16[8,256,256]{2,0,1:T(8,128)(2,1)} %copy.35), calls=%async_computation.2 | async-start | bytes 2097152 | tf_op jit(solution)/shard_map/all_to_all | solution.py:78
  112.7 11.6 %fusion.10 = f32[32,64,1024]{2,0,1:T(8,128)} fusion(bf16[8,32,1]{1,0,2:T(8,128)(2,1)S(1)} %fusion.12, bf16[32,64,1024]{2,1,0:T(8,128)(2,1)} %param.7, bf16[8,64,1024]{2,1,0:T(8,128)(2,1)} %param.11), kind=kOutput, calls=%fused_computation.14 | convolution fusion | flops 68681728 | bytes 13632000 | tf_op jit(solution)/shard_map/mq,mrc->qrc/dot_general | solution.py:36
  124.3 1.6 %copy.41 = bf16[56,64,256]{2,1,0:T(8,128)(2,1)} copy(bf16[56,64,256]{2,0,1:T(8,128)(2,1)S(1)} %subtract_convert_fusion) | data formatting | bytes 3670016
  125.9 0.9 all-to-all-done.2
  127.1 11.1 %fusion.2 = bf16[32,64,1024]{2,1,0:T(8,128)(2,1)} fusion(f32[32,64,1024]{2,0,1:T(8,128)} %fusion.10, bf16[32,64,1024]{2,1,0:T(8,128)(2,1)} %param.7, bf16[32,64,256]{2,1,0:T(8,128)(2,1)S(1)} %bitcast.37, bf16[1024,256,1]{1,0,2:T(8,128)(2,1)S(1)} %copy-done.1), kind=kOutput, calls=%fused_computation.3 | convolution fusion | flops 1084227584 | bytes 18350080 | tf_op jit(solution)/shard_map/qrj,cj->qrc/dot_general | solution.py:36
  (17 shorter events, 1.3 us)
Async XLA Ops:
  7.2 49.4 %copy-start = (bf16[224,32]{0,1:T(8,128)(2,1)S(1)}, bf16[224,32]{0,1:T(8,128)(2,1)}, u32[]{:S(2)}) copy-start(bf16[224,32]{0,1:T(8,128)(2,1)} %param.8) | copy-start | bytes 43012
  7.2 49.4 %all-gather.2.cloned.1.call-start = ((), (), s32[]{:S(2)}) async-start(), calls=%async_computation.3 | async-start | bytes 1310720 | tf_op jit(solution)/shard_map/all_gather | solution.py:67
  10.8 17.3 %copy-start.2 = (bf16[256,128,1]{0,1,2:T(8,128)(2,1)S(1)}, bf16[256,128,1]{0,1,2:T(8,128)(2,1)}, u32[]{:S(2)}) copy-start(bf16[256,128,1]{0,1,2:T(8,128)(2,1)} %constant.28) | copy-start | bytes 196612
  28.5 7.8 %collective-permute-start = (bf16[8,32,256]{2,1,0:T(8,128)(2,1)S(1)}, bf16[8,32,256]{2,1,0:T(8,128)(2,1)S(1)}, u32[]{:S(2)}, u32[]{:S(2)}) collective-permute-start(bf16[8,32,256]{2,1,0:T(8,128)(2,1)S(1)} %get-tuple-element.10), channel_id=1, source_target_pairs={{0,4},{4,8},{8,12},{12,16},{16,20},{20,24},{24,28},{1,5},{5,9},{9,... | collective-permute-start | bytes 393224 | tf_op jit(solution)/shard_map/ppermute | solution.py:59
  31.9 7.1 %collective-permute-start.1 = (bf16[8,32,256]{2,1,0:T(8,128)(2,1)S(1)}, bf16[8,32,256]{2,1,0:T(8,128)(2,1)S(1)}, u32[]{:S(2)}, u32[]{:S(2)}) collective-permute-start(bf16[8,32,256]{2,1,0:T(8,128)(2,1)S(1)} %get-tuple-element.11), channel_id=1, source_target_pairs={{4,0},{8,4},{12,8},{16,12},{20,16},{24,20},{28,24},{5,1},{9,5},{13... | collective-permute-start | bytes 393224 | tf_op jit(solution)/shard_map/ppermute | solution.py:58
  78.9 33.7 %copy-start.3 = (bf16[8,224]{1,0:T(8,128)(2,1)S(1)}, bf16[8,224]{1,0:T(8,128)(2,1)}, u32[]{:S(2)}) copy-start(bf16[8,224]{1,0:T(8,128)(2,1)} %param.9) | copy-start | bytes 10756
  79.1 25.4 %collective-permute-start.2 = (bf16[8,32,256]{1,2,0:T(8,128)(2,1)S(1)}, bf16[8,32,256]{1,2,0:T(8,128)(2,1)S(1)}, u32[]{:S(2)}, u32[]{:S(2)}) collective-permute-start(bf16[8,32,256]{1,2,0:T(8,128)(2,1)S(1)} %get-tuple-element.8), channel_id=1, source_target_pairs={{0,4},{4,8},{8,12},{12,16},{16,20},{20,24},{24,28},{1,5},{5,9},{9,... | collective-permute-start | bytes 393224 | tf_op jit(solution)/shard_map/ppermute | solution.py:75
  82.5 23.9 %collective-permute-start.3 = (bf16[8,32,256]{1,2,0:T(8,128)(2,1)S(1)}, bf16[8,32,256]{1,2,0:T(8,128)(2,1)S(1)}, u32[]{:S(2)}, u32[]{:S(2)}) collective-permute-start(bf16[8,32,256]{1,2,0:T(8,128)(2,1)S(1)} %get-tuple-element.9), channel_id=1, source_target_pairs={{4,0},{8,4},{12,8},{16,12},{20,16},{24,20},{28,24},{5,1},{9,5},{13... | collective-permute-start | bytes 393224 | tf_op jit(solution)/shard_map/ppermute | solution.py:74
  108.9 18.0 %all-to-all-start.2 = ((bf16[8,256,256]{2,0,1:T(8,128)(2,1)}), bf16[8,256,256]{2,0,1:T(8,128)(2,1)S(1)}, u32[]{:S(2)}, u32[]{:S(2)}) async-start(bf16[8,256,256]{2,0,1:T(8,128)(2,1)} %copy.35), calls=%async_computation.2 | async-start | bytes 2097152 | tf_op jit(solution)/shard_map/all_to_all | solution.py:78
  124.3 2.8 %copy-start.1 = (bf16[1024,256,1]{1,0,2:T(8,128)(2,1)S(1)}, bf16[1024,256,1]{1,0,2:T(8,128)(2,1)}, u32[]{:S(2)}) copy-start(bf16[1024,256,1]{1,0,2:T(8,128)(2,1)} %constant.27) | copy-start | bytes 1572868
Sparse Core Ops, SparseCore 0:
  40.0 16.5 all-gather.1

commit v2 on v1

--- a/solution.py
+++ b/solution.py
@@ -2,6 +2,8 @@
 import jax.numpy as jnp
 import numpy as np
 from jax import lax
+from jax.experimental import pallas as pl
+from jax.experimental.pallas import tpu as pltpu
 from jax.sharding import PartitionSpec as P
 
 DECIM = 4
@@ -36,7 +38,7 @@
     return jnp.einsum(spec, a, b, preferred_element_type=jnp.float32)
 
 
-def shards(latent, basis, response, hyper_obs, multi_obs):
+def shards_plain(latent, basis, response, hyper_obs, multi_obs):
     bf16 = jnp.bfloat16
     f32 = jnp.float32
     group = hyper_obs.shape[0]
@@ -84,6 +86,402 @@
     return (z_next, hs_residual)
 
 
+N_SPEC = 4
+SLAB = 64
+WINDOW = 96
+LANES = 128
+MESH = pl.DeviceIdType.MESH
+bf16 = jnp.bfloat16
+f32 = jnp.float32
+
+
+def mm(a, b):
+    return jnp.dot(a, b, preferred_element_type=f32)
+
+
+def mm_nt(a, b):
+    return lax.dot_general(a, b, (((1,), (1,)), ((), ())), preferred_element_type=f32)
+
+
+def same(shape, row_of, col_of):
+    rows = row_of(lax.broadcasted_iota(jnp.int32, shape, 0))
+    cols = col_of(lax.broadcasted_iota(jnp.int32, shape, 1))
+    return jnp.where(rows == cols, 1.0, 0.0)
+
+
+def low(i):
+    return i & 15
+
+
+def high(i):
+    return i >> 4
+
+
+def plain(i):
+    return i
+
+
+def joined(
+    lat_hbm, mo_hbm, hy_hbm, basis, repeated, kc, kct, kri, krt,
+    z_hbm, hs_hbm,
+    lat, mo, hy, z, hs, base, msr, kb, kbt, km, kmt,
+    s_a, r_a, own, s_h, r_h, s_x, r_x, blur, s_b, r_b, own_b, s_y, r_y, wide,
+    in_sem, out_sem, send_sem, recv_sem,
+):
+    t = lax.axis_index("tile")
+    s = lax.axis_index("spec")
+    count = lax.axis_size("tile")
+    x, core = s // 2, s % 2
+    half = lat.shape[0] // 2
+    partner = (t, 2 * x + 1 - core)
+    peer = (t, 2 * (1 - x) + core)
+    fwd, bwd = t - 1 + 2 * x, t + 1 - 2 * x
+    has_fwd = jnp.logical_and(fwd >= 0, fwd < count)
+    has_bwd = jnp.logical_and(bwd >= 0, bwd < count)
+    mine = pl.multiple_of(half * core, half)
+    other = pl.multiple_of(half * (1 - core), half)
+    edge = pl.multiple_of(64 * x, 32)
+    far = pl.multiple_of(64 * (1 - x), 32)
+    tile0 = pl.multiple_of(32 * (1 - x), 32)
+    part0 = pl.multiple_of(32 * x, 32)
+    part1 = pl.multiple_of(32 * (1 - x), 32)
+
+    loads = [
+        pltpu.make_async_copy(
+            lat_hbm.at[pl.ds(other, half)], lat.at[pl.ds(other, half)], in_sem.at[0]
+        ),
+        pltpu.make_async_copy(
+            lat_hbm.at[pl.ds(mine, half)], lat.at[pl.ds(mine, half)], in_sem.at[1]
+        ),
+        pltpu.make_async_copy(mo_hbm, mo, in_sem.at[2]),
+        pltpu.make_async_copy(hy_hbm, hy, in_sem.at[3]),
+    ]
+    for load in loads:
+        load.start()
+
+    barrier = pltpu.get_barrier_semaphore()
+    pl.semaphore_signal(barrier, inc=1, device_id=partner, device_id_type=MESH)
+    pl.semaphore_signal(barrier, inc=1, device_id=peer, device_id_type=MESH)
+
+    @pl.when(has_fwd)
+    def _():
+        pl.semaphore_signal(barrier, inc=1, device_id=(fwd, s), device_id_type=MESH)
+
+    @pl.when(has_bwd)
+    def _():
+        pl.semaphore_signal(barrier, inc=1, device_id=(bwd, s), device_id_type=MESH)
+
+    def remote(kind, c, src, dst, device):
+        return pltpu.make_async_remote_copy(
+            src_ref=src,
+            dst_ref=dst,
+            send_sem=send_sem.at[kind, c],
+            recv_sem=recv_sem.at[kind, c],
+            device_id=device,
+            device_id_type=MESH,
+        )
+
+    def both(c):
+        return slice(c * LANES, (c + 1) * LANES)
+
+    copy_a = [remote(0, c, s_a.at[c], r_a.at[c], partner) for c in range(2)]
+    copy_h = [remote(1, c, s_h.at[c], r_h.at[c], (fwd, s)) for c in range(2)]
+    copy_x0 = [remote(2, c, s_x.at[c, 0], r_x.at[c, 0], peer) for c in range(2)]
+    copy_x1 = [remote(3, c, s_x.at[c, 1], r_x.at[c, 1], peer) for c in range(2)]
+    copy_c = [remote(4, c, blur.at[c, core], blur.at[c, core], partner) for c in range(2)]
+    copy_b = [remote(5, c, s_b.at[c], r_b.at[c], partner) for c in range(2)]
+    copy_y0 = [remote(6, c, s_y.at[c, 0], r_y.at[c, 0], peer) for c in range(2)]
+    copy_y1 = [remote(7, c, s_y.at[c, 1], r_y.at[c, 1], peer) for c in range(2)]
+    copy_g = [
+        remote(
+            8, c, wide.at[c, core, :, pl.ds(far, 32)], wide.at[c, core, :, pl.ds(edge, 32)], (bwd, s)
+        )
+        for c in range(2)
+    ]
+    copy_d = [
+        remote(
+            9, c, wide.at[c, core, :, pl.ds(tile0, 64)], wide.at[c, core, :, pl.ds(tile0, 64)], partner
+        )
+        for c in range(2)
+    ]
+    copy_e = [
+        remote(
+            10, c, wide.at[c, core, :, pl.ds(edge, 32)], wide.at[c, core, :, pl.ds(edge, 32)], partner
+        )
+        for c in range(2)
+    ]
+
+    def partial(first, g):
+        cells = lat[pl.ds(first + 4 * g, 4)].reshape(4 * SLAB, -1)
+        narrow = mm(cells, kc[...]).astype(bf16)
+        return mm(kri[core], narrow).reshape(4, WINDOW, 2 * LANES)
+
+    loads[0].wait()
+
+    @pl.loop(0, half // 4)
+    def _(g):
+        part = partial(other, g).astype(bf16)
+        for c in range(2):
+            s_a[c, pl.ds(4 * g, 4)] = part[:, :, both(c)]
+
+    pl.semaphore_wait(barrier, 2 + has_fwd.astype(jnp.int32) + has_bwd.astype(jnp.int32))
+    for c in range(2):
+        copy_a[c].start()
+    loads[1].wait()
+
+    @pl.loop(0, half // 4)
+    def _(g):
+        part = partial(mine, g)
+        for c in range(2):
+            own[c, pl.ds(4 * g, 4)] = part[:, :, both(c)]
+
+    for c in range(2):
+        copy_a[c].wait_recv()
+        s_h[c] = (own[c, :, pl.ds(edge, 32)] + r_a[c, :, pl.ds(edge, 32)].astype(f32)).astype(bf16)
+
+        @pl.when(has_fwd)
+        def _():
+            copy_h[c].start()
+
+        mid = own[c, :, 32:64] + r_a[c, :, 32:64].astype(f32)
+        own[c, :, 32:64] = mid
+        s_x[c, 0] = mid.astype(bf16)
+        copy_x0[c].start()
+        own[c, :, pl.ds(far, 32)] = own[c, :, pl.ds(far, 32)] + r_a[c, :, pl.ds(far, 32)].astype(f32)
+
+    bands = hy.shape[0]
+    lead = lat.shape[0] * 16
+    spread_q = same((lat.shape[0], lead), plain, high).astype(bf16)
+    spread_qt = same((lead, lat.shape[0]), high, plain).astype(bf16)
+    pick = same((bands * 16, basis.shape[0]), lambda i: (i >> 4) + bands * s, plain).astype(bf16)
+    pick_t = same((basis.shape[0], bands * 16), plain, lambda i: (i >> 4) + bands * s).astype(bf16)
+    tall = mm_nt(spread_qt, basis[...]).astype(bf16)
+    picked = mm(pick, basis[...]).astype(bf16)
+    kb[...] = (mm(picked, spread_q) * same((bands * 16, lead), low, low)).astype(bf16)
+    kbt[...] = (mm(tall, pick_t) * same((lead, bands * 16), low, low)).astype(bf16)
+    mixed = mm(repeated[...], basis[...]).astype(bf16)
+    km[...] = (mm(mixed, spread_q) * same((LANES, lead), low, low)).astype(bf16)
+    kmt[...] = (mm_nt(tall, repeated[...]) * same((lead, LANES), low, low)).astype(bf16)
+
+    for c in range(2):
+
+        @pl.when(has_bwd)
+        def _():
+            copy_h[c].wait_recv()
+            own[c, :, pl.ds(far, 32)] = own[c, :, pl.ds(far, 32)] + r_h[c].astype(f32)
+
+        s_x[c, 1] = own[c, :, pl.ds(far, 32)].astype(bf16)
+        copy_x1[c].start()
+
+    loads[2].wait()
+
+    @pl.loop(0, SLAB // 16)
+    def _(g):
+        at = pl.ds(pl.multiple_of(16 * g, 16), 16)
+        for n in range(lat.shape[2] // 256):
+            cut = slice(256 * n, 256 * n + 256)
+            cells = lat[:, at, cut].reshape(lead, 256)
+            resid = mm(km[...], cells) - mo[:, at, cut].reshape(LANES, 256).astype(f32)
+            back = mm(kmt[...], resid.astype(bf16))
+            base[:, at, cut] = (cells.astype(f32) - STEP * back).reshape(-1, 16, 256)
+
+    for c in range(2):
+        copy_x0[c].wait_recv()
+        blur[c, core, :, pl.ds(part1, 32)] = (
+            own[c, :, pl.ds(far, 32)] + r_x[c, 0].astype(f32)
+        ).astype(bf16)
+        copy_x1[c].wait_recv()
+        blur[c, core, :, pl.ds(part0, 32)] = (own[c, :, 32:64] + r_x[c, 1].astype(f32)).astype(bf16)
+        copy_c[c].start()
+
+    loads[3].wait()
+    stores = []
+    for c in range(2):
+        copy_c[c].wait()
+
+        @pl.loop(0, SLAB // 16)
+        def _(g):
+            at = pl.ds(pl.multiple_of(16 * g, 16), 16)
+            cells = blur[c, :, :, at].reshape(lead, LANES)
+            resid = mm(kb[...], cells) - hy[:, at, both(c)].reshape(bands * 16, LANES).astype(f32)
+            resid = resid.astype(bf16)
+            hs[:, at, both(c)] = resid.reshape(bands, 16, LANES)
+            given = mm(kbt[pl.ds(16 * other, 16 * half)], resid)
+            s_b[c, :, at] = given.astype(bf16).reshape(half, 16, LANES)
+            kept = mm(kbt[pl.ds(16 * mine, 16 * half)], resid)
+            own_b[c, :, at] = kept.reshape(half, 16, LANES)
+
+        copy_b[c].start()
+
+    stores.append(pltpu.make_async_copy(hs, hs_hbm, out_sem.at[8]))
+    stores[0].start()
+
+    for c in range(2):
+        copy_b[c].wait_recv()
+        total = own_b[c] + r_b[c].astype(f32)
+        own_b[c] = total
+        s_y[c, 0] = own_b[c, :, pl.ds(part0, 32)].astype(bf16)
+        copy_y0[c].start()
+        s_y[c, 1] = own_b[c, :, pl.ds(part1, 32)].astype(bf16)
+        copy_y1[c].start()
+
+    for c in range(2):
+        copy_y0[c].wait_recv()
+        wide[c, core, :, pl.ds(far, 32)] = (
+            own_b[c, :, pl.ds(part1, 32)] + r_y[c, 0].astype(f32)
+        ).astype(bf16)
+
+        @pl.when(has_bwd)
+        def _():
+            copy_g[c].start()
+
+        copy_y1[c].wait_recv()
+        wide[c, core, :, 32:64] = (own_b[c, :, pl.ds(part0, 32)] + r_y[c, 1].astype(f32)).astype(bf16)
+        copy_d[c].start()
+
+    for c in range(2):
+
+        @pl.when(has_fwd)
+        def _():
+            copy_g[c].wait_recv()
+
+        @pl.when(jnp.logical_not(has_fwd))
+        def _():
+            wide[c, core, :, pl.ds(edge, 32)] = jnp.zeros((half, 32, LANES), bf16)
+
+        copy_e[c].start()
+
+    def finish(first, who, slot):
+        def group(g, carry):
+            cells = jnp.concatenate(
+                [wide[c, who, pl.ds(4 * g, 4)].reshape(4 * WINDOW, LANES) for c in range(2)], axis=1
+            )
+            rows = mm(krt[core], cells).astype(bf16)
+            at = pl.ds(first + 4 * g, 4)
+            for n in range(lat.shape[2] // 256):
+                cut = slice(256 * n, 256 * n + 256)
+                back = mm(rows, kct[:, cut]).reshape(4, SLAB, 256)
+                z[at, :, cut] = (base[at, :, cut] - STEP * back).astype(bf16)
+            return carry
+
+        lax.fori_loop(0, half // 4, group, 0)
+        store = pltpu.make_async_copy(
+            z.at[pl.ds(first, half)], z_hbm.at[pl.ds(first, half)], out_sem.at[slot]
+        )
+        store.start()
+        stores.append(store)
+
+    finish(mine, core, 0)
+    for c in range(2):
+        copy_d[c].wait_recv()
+        copy_e[c].wait_recv()
+    finish(other, 1 - core, 1)
+
+    for c in range(2):
+        for copies in (copy_a, copy_x0, copy_x1, copy_b, copy_y0, copy_y1, copy_d, copy_e):
+            copies[c].wait_send()
+
+        @pl.when(has_fwd)
+        def _():
+            copy_h[c].wait_send()
+
+        @pl.when(has_bwd)
+        def _():
+            copy_g[c].wait_send()
+
+    for store in stores:
+        store.wait()
+
+
+def row_window(core):
+    return kernel_values(
+        SLAB * core + np.arange(SLAB)[None, :] - DECIM * np.arange(WINDOW)[:, None] + HALO
+    )
+
+
+def shards_joined(latent, basis, response, hyper_obs, multi_obs):
+    cols = column_matrix(latent.shape[2])
+    row = np.stack([np.kron(np.eye(4, dtype=np.float32), row_window(c).astype(np.float32)) for c in (0, 1)])
+    row = row.astype(bf16)
+    lead = latent.shape[0] * 16
+    bands = hyper_obs.shape[0] * 16
+    half = latent.shape[0] // 2
+    coarse, low_cols = hyper_obs.shape[1:]
+
+    def buf(shape, dtype=bf16):
+        return pltpu.VMEM(shape, dtype)
+
+    any_spec = pl.BlockSpec(memory_space=pl.ANY)
+    vmem_spec = pl.BlockSpec(memory_space=pltpu.VMEM)
+    return pl.pallas_call(
+        joined,
+        out_shape=(
+            jax.ShapeDtypeStruct(latent.shape, bf16),
+            jax.ShapeDtypeStruct(hyper_obs.shape, bf16),
+        ),
+        in_specs=[any_spec] * 3 + [vmem_spec] * 6,
+        out_specs=(any_spec, any_spec),
+        scratch_shapes=[
+            buf(latent.shape),
+            buf(multi_obs.shape),
+            buf(hyper_obs.shape),
+            buf(latent.shape),
+            buf(hyper_obs.shape),
+            buf(latent.shape, f32),
+            buf((8, LANES)),
+            buf((bands, lead)),
+            buf((lead, bands)),
+            buf((LANES, lead)),
+            buf((lead, LANES)),
+            buf((2, half, WINDOW, LANES)),
+            buf((2, half, WINDOW, LANES)),
+            buf((2, half, WINDOW, LANES), f32),
+            buf((2, half, 32, LANES)),
+            buf((2, half, 32, LANES)),
+            buf((2, 2, half, 32, LANES)),
+            buf((2, 2, half, 32, LANES)),
+            buf((2, 2, half, coarse, LANES)),
+            buf((2, half, coarse, LANES)),
+            buf((2, half, coarse, LANES)),
+            buf((2, half, coarse, LANES), f32),
+            buf((2, 2, half, 32, LANES)),
+            buf((2, 2, half, 32, LANES)),
+            buf((2, 2, half, WINDOW, LANES)),
+            pltpu.SemaphoreType.DMA((4,)),
+            pltpu.SemaphoreType.DMA((9,)),
+            pltpu.SemaphoreType.DMA((11, 2)),
+            pltpu.SemaphoreType.DMA((11, 2)),
+        ],
+        compiler_params=pltpu.CompilerParams(
+            collective_id=0, has_side_effects=True, vmem_limit_bytes=56 * 1024 * 1024
+        ),
+        cost_estimate=pl.CostEstimate(
+            flops=10 * 1024**3, bytes_accessed=13 * 1024 * 1024, transcendentals=0
+        ),
+        name="joined",
+    )(
+        latent,
+        multi_obs,
+        hyper_obs,
+        basis,
+        jnp.repeat(response, 16, axis=0),
+        jnp.asarray(cols),
+        jnp.asarray(cols.T),
+        jnp.asarray(row),
+        jnp.asarray(row.transpose(0, 2, 1)),
+    )
+
+
+def shards(latent, basis, response, hyper_obs, multi_obs):
+    fits = (
+        lax.axis_size("spec") == N_SPEC
+        and latent.shape == (32, SLAB, 1024)
+        and hyper_obs.shape[1:] == (SLAB, 2 * LANES)
+    )
+    run = shards_joined if fits else shards_plain
+    return run(latent, basis, response, hyper_obs, multi_obs)
+
+
 def solution(mesh):
     in_specs = (
         P(None, ("tile", "spec"), None),

time: 145 us -> 61 us (0.42)
  Pallas kernels: 0 us -> 50.8 us
  waiting for transfers between devices: 42 us -> 0 us
  blocking collectives: 34 us -> 0 us
  matrix products: 31.6 us -> 0 us
  starting transfers between devices: 17.2 us -> 0 us
  between operations: 14.2 us -> 0.65 us
  local copies, waits for them, and re-layouts: 4.91 us -> 9.04 us
    pallas_call x0 -> x1, Pallas kernels: none -> 50.8 us  [shards_joined(): pl.pallas_call(joined, out_shape=(jax.ShapeDtypeStruct(latent.shape, bf16...]
    all_to_all x2 -> x0, blocking collectives: 34 us -> none  [the longest x1 17.2 us: shards(): lax.all_to_all(narrow, 'spec', split_axis=0, concat_axis=1, tiled=True)]
    dot_general x8 -> x0, matrix products: 31.6 us -> none  [dot(): return jnp.einsum(spec, a, b, preferred_element_type=jnp.float32)]
    ppermute x4 -> x0, waiting for transfers between devices: 24.4 us -> none  [the longest x1 18.7 us: shards(): from_above = lax.ppermute(back[:, coarse - RIM:], 'tile', down)]
    all_gather x1 -> x0, waiting for transfers between devices: 16.7 us -> none  [shards(): blurred = lax.all_gather(own, 'spec', axis=0, tiled=True)]
    ppermute x4 -> x0, starting transfers between devices: 13.5 us -> none  [the longest x1 3.43 us: shards(): below = lax.ppermute(part[:, RIM + coarse:].astype(bf16), 'tile', down)]
    unnamed x9 -> x5, local copies, waits for them, and re-layouts: 1.67 us -> 7.72 us
    all_to_all x1 -> x0, starting transfers between devices: 3.7 us -> none  [shards(): lax.all_to_all(rows_back, 'spec', split_axis=1, concat_axis=0, tiled=True)]
  transfers between devices with their start and end apart: 6 -> 0, of which waited for: 6 -> 0; matrix products, arithmetic and copies ran while one was open for 9% -> 0% of each run, Pallas kernels for 0% -> 0%
where the time goes in v2:
time: 61 us; the launch traced here: 60.5 us
  Pallas kernels  50.8 us (83%)
  local copies, waits for them, and re-layouts  9.04 us (15%)
  between operations  0.65 us (1%)
    pallas_call x1, Pallas kernels, shards_joined(): pl.pallas_call(joined, out_shape=(jax.ShapeDtypeStruct(latent.shape, bf16...  50.8 us
    unnamed x5, local copies, waits for them, and re-layouts  7.72 us
    broadcast_in_dim x1, local copies, waits for them, and re-layouts, shards_joined(): jnp.repeat(response, 16, axis=0)  1.32 us

profile of v2, /device:TPU:8, one launch (start us, length us, event | category | flops | bytes accessed | tf_op | source)
XLA Modules:
  0.0 60.5 jit_solution(1803525945819685389)
XLA Ops:
  0.6 1.4 %copy.11.basis = bf16[224,32]{1,0:T(8,128)(2,1)} copy(bf16[224,32]{0,1:T(8,128)(2,1)} %param.10) | data formatting | bytes 28672 | tf_op args[1]
  2.1 1.3 %broadcast_in_dim.3 = bf16[8,16,224]{2,1,0:T(8,128)(2,1)} broadcast(bf16[8,224]{1,0:T(8,128)(2,1)} %param.11), dimensions={0,2} | broadcast | bytes 60928 | tf_op jit(solution)/shard_map/broadcast_in_dim | solution.py:467
  3.4 50.8 %joined.1 = (bf16[32,64,1024]{2,1,0:T(8,128)(2,1)}, bf16[56,64,256]{2,1,0:T(8,128)(2,1)}) custom-call(bf16[32,64,1024]{2,1,0:T(8,128)(2,1)} %lat_hbm.1, bf16[8,64,1024]{2,1,0:T(8,128)(2,1)} %mo_hbm.1, bf16[56,64,256]{2,1,0:T(8,128)(2,1)} %hy_hbm.1, bf16[224,32]{1,0:T(8,128)(2,1)} %copy.11.basis, bf16[128,224]{1,0:T(8,128)(2,1)} %bitcast.1, ...), custom_call_target="tpu_custom_call" | custom-call | flops 10737418240 | bytes 13631488 | tf_op jit(solution)/shard_map/joined/pallas_call | solution.py:416
  54.2 0.0 copy-start
  54.2 5.0 %copy.14 = bf16[32,64,1024]{2,1,0:T(8,128)(2,1)} copy(bf16[32,64,1024]{2,1,0:T(8,128)(2,1)} %get-tuple-element.4) | data formatting | bytes 8388608
  59.3 0.0 copy-done
  59.3 1.2 %copy.15 = bf16[56,64,256]{2,1,0:T(8,128)(2,1)} copy(bf16[56,64,256]{2,1,0:T(8,128)(2,1)S(1)} %copy-done) | data formatting | bytes 3670016
Async XLA Ops:
  54.2 5.1 %copy-start = (bf16[56,64,256]{2,1,0:T(8,128)(2,1)S(1)}, bf16[56,64,256]{2,1,0:T(8,128)(2,1)}, u32[]{:S(2)}) copy-start(bf16[56,64,256]{2,1,0:T(8,128)(2,1)} %get-tuple-element.5) | copy-start | bytes 5505028

commit v3 on v2

--- a/solution.py
+++ b/solution.py
@@ -122,9 +122,9 @@
 
 
 def joined(
-    lat_hbm, mo_hbm, hy_hbm, basis, repeated, kc, kct, kri, krt,
+    lat_hbm, mo_hbm, hy_hbm, basis_t, response, kc, kct, kri, krt,
     z_hbm, hs_hbm,
-    lat, mo, hy, z, hs, base, msr, kb, kbt, km, kmt,
+    lat, mo, hy, z, hs, base, kb, kbt, km, kmt, ks,
     s_a, r_a, own, s_h, r_h, s_x, r_x, blur, s_b, r_b, own_b, s_y, r_y, wide,
     in_sem, out_sem, send_sem, recv_sem,
 ):
@@ -156,7 +156,7 @@
         pltpu.make_async_copy(mo_hbm, mo, in_sem.at[2]),
         pltpu.make_async_copy(hy_hbm, hy, in_sem.at[3]),
     ]
-    for load in loads:
+    for load in (loads[3], loads[0], loads[1], loads[2]):
         load.start()
 
     barrier = pltpu.get_barrier_semaphore()
@@ -190,23 +190,22 @@
     copy_x1 = [remote(3, c, s_x.at[c, 1], r_x.at[c, 1], peer) for c in range(2)]
     copy_c = [remote(4, c, blur.at[c, core], blur.at[c, core], partner) for c in range(2)]
     copy_b = [remote(5, c, s_b.at[c], r_b.at[c], partner) for c in range(2)]
-    copy_y0 = [remote(6, c, s_y.at[c, 0], r_y.at[c, 0], peer) for c in range(2)]
-    copy_y1 = [remote(7, c, s_y.at[c, 1], r_y.at[c, 1], peer) for c in range(2)]
+    copy_y = [remote(6, c, s_y.at[c], r_y.at[c], peer) for c in range(2)]
     copy_g = [
         remote(
-            8, c, wide.at[c, core, :, pl.ds(far, 32)], wide.at[c, core, :, pl.ds(edge, 32)], (bwd, s)
+            7, c, wide.at[c, core, :, pl.ds(far, 32)], wide.at[c, core, :, pl.ds(edge, 32)], (bwd, s)
         )
         for c in range(2)
     ]
     copy_d = [
         remote(
-            9, c, wide.at[c, core, :, pl.ds(tile0, 64)], wide.at[c, core, :, pl.ds(tile0, 64)], partner
+            8, c, wide.at[c, core, :, pl.ds(tile0, 64)], wide.at[c, core, :, pl.ds(tile0, 64)], partner
         )
         for c in range(2)
     ]
     copy_e = [
         remote(
-            10, c, wide.at[c, core, :, pl.ds(edge, 32)], wide.at[c, core, :, pl.ds(edge, 32)], partner
+            9, c, wide.at[c, core, :, pl.ds(edge, 32)], wide.at[c, core, :, pl.ds(edge, 32)], partner
         )
         for c in range(2)
     ]
@@ -215,6 +214,32 @@
         cells = lat[pl.ds(first + 4 * g, 4)].reshape(4 * SLAB, -1)
         narrow = mm(cells, kc[...]).astype(bf16)
         return mm(kri[core], narrow).reshape(4, WINDOW, 2 * LANES)
+
+    bands = hy.shape[0]
+    lead = lat.shape[0] * 16
+    all_bands = basis_t.shape[1]
+    spread_q = same((lat.shape[0], lead), plain, high).astype(bf16)
+    spread_qt = same((lead, lat.shape[0]), high, plain).astype(bf16)
+    tall = mm(spread_qt, basis_t[...]).astype(bf16)
+    pick_t = same((all_bands, bands * 16), plain, lambda i: (i >> 4) + bands * s).astype(bf16)
+    kbt[...] = (mm(tall, pick_t) * same((lead, bands * 16), low, low)).astype(bf16)
+
+    loads[3].wait()
+
+    def observed(at, width):
+        return hy[:, at, width].reshape(bands * 16, -1)
+
+    @pl.loop(0, SLAB // 16)
+    def _(g):
+        at = pl.ds(pl.multiple_of(16 * g, 16), 16)
+        given = mm(kbt[pl.ds(16 * other, 16 * half)], observed(at, slice(None)))
+        given = given.astype(bf16).reshape(half, 16, 2 * LANES)
+        for c in range(2):
+            s_b[c, :, at] = given[:, :, both(c)]
+
+    pl.semaphore_wait(barrier, 2 + has_fwd.astype(jnp.int32) + has_bwd.astype(jnp.int32))
+    for c in range(2):
+        copy_b[c].start()
 
     loads[0].wait()
 
@@ -224,9 +249,25 @@
         for c in range(2):
             s_a[c, pl.ds(4 * g, 4)] = part[:, :, both(c)]
 
-    pl.semaphore_wait(barrier, 2 + has_fwd.astype(jnp.int32) + has_bwd.astype(jnp.int32))
     for c in range(2):
         copy_a[c].start()
+
+    @pl.loop(0, SLAB // 16)
+    def _(g):
+        at = pl.ds(pl.multiple_of(16 * g, 16), 16)
+        kept = mm(kbt[pl.ds(16 * mine, 16 * half)], observed(at, slice(None)))
+        kept = kept.reshape(half, 16, 2 * LANES)
+        for c in range(2):
+            own_b[c, :, at] = kept[:, :, both(c)]
+
+    def share(c):
+        copy_b[c].wait_recv()
+        total = own_b[c] + r_b[c].astype(f32)
+        own_b[c] = total
+        s_y[c] = total.astype(bf16)
+        copy_y[c].start()
+
+    share(0)
     loads[1].wait()
 
     @pl.loop(0, half // 4)
@@ -249,19 +290,22 @@
         copy_x0[c].start()
         own[c, :, pl.ds(far, 32)] = own[c, :, pl.ds(far, 32)] + r_a[c, :, pl.ds(far, 32)].astype(f32)
 
-    bands = hy.shape[0]
-    lead = lat.shape[0] * 16
-    spread_q = same((lat.shape[0], lead), plain, high).astype(bf16)
-    spread_qt = same((lead, lat.shape[0]), high, plain).astype(bf16)
-    pick = same((bands * 16, basis.shape[0]), lambda i: (i >> 4) + bands * s, plain).astype(bf16)
-    pick_t = same((basis.shape[0], bands * 16), plain, lambda i: (i >> 4) + bands * s).astype(bf16)
-    tall = mm_nt(spread_qt, basis[...]).astype(bf16)
-    picked = mm(pick, basis[...]).astype(bf16)
+    pick = same((bands * 16, all_bands), lambda i: (i >> 4) + bands * s, plain).astype(bf16)
+    repeated = jnp.broadcast_to(
+        response[...].astype(f32)[:, None, :], (response.shape[0], 16, all_bands)
+    )
+    repeated = repeated.reshape(LANES, all_bands).astype(bf16)
+    picked = mm_nt(pick, basis_t[...]).astype(bf16)
     kb[...] = (mm(picked, spread_q) * same((bands * 16, lead), low, low)).astype(bf16)
-    kbt[...] = (mm(tall, pick_t) * same((lead, bands * 16), low, low)).astype(bf16)
-    mixed = mm(repeated[...], basis[...]).astype(bf16)
+    mixed = mm_nt(repeated, basis_t[...]).astype(bf16)
     km[...] = (mm(mixed, spread_q) * same((LANES, lead), low, low)).astype(bf16)
-    kmt[...] = (mm_nt(tall, repeated[...]) * same((lead, LANES), low, low)).astype(bf16)
+    kmt[...] = (mm_nt(tall, repeated) * same((lead, LANES), low, low)).astype(bf16)
+    square = mm_nt(basis_t[...], basis_t[...])
+    first = square.astype(bf16)
+    second = (square - first.astype(f32)).astype(bf16)
+    for k, part in enumerate((first, second)):
+        grown = mm(mm(spread_qt, part).astype(bf16), spread_q)
+        ks[k] = (grown * same((lead, lead), low, low)).astype(bf16)
 
     for c in range(2):
 
@@ -273,6 +317,7 @@
         s_x[c, 1] = own[c, :, pl.ds(far, 32)].astype(bf16)
         copy_x1[c].start()
 
+    share(1)
     loads[2].wait()
 
     @pl.loop(0, SLAB // 16)
@@ -294,50 +339,37 @@
         blur[c, core, :, pl.ds(part0, 32)] = (own[c, :, 32:64] + r_x[c, 1].astype(f32)).astype(bf16)
         copy_c[c].start()
 
-    loads[3].wait()
     stores = []
     for c in range(2):
         copy_c[c].wait()
+        copy_y[c].wait_recv()
 
         @pl.loop(0, SLAB // 16)
         def _(g):
             at = pl.ds(pl.multiple_of(16 * g, 16), 16)
             cells = blur[c, :, :, at].reshape(lead, LANES)
-            resid = mm(kb[...], cells) - hy[:, at, both(c)].reshape(bands * 16, LANES).astype(f32)
-            resid = resid.astype(bf16)
-            hs[:, at, both(c)] = resid.reshape(bands, 16, LANES)
-            given = mm(kbt[pl.ds(16 * other, 16 * half)], resid)
-            s_b[c, :, at] = given.astype(bf16).reshape(half, 16, LANES)
-            kept = mm(kbt[pl.ds(16 * mine, 16 * half)], resid)
-            own_b[c, :, at] = kept.reshape(half, 16, LANES)
-
-        copy_b[c].start()
+            rows = pl.ds(16 * mine, 16 * half)
+            total = mm(ks[0, rows], cells) + mm(ks[1, rows], cells)
+            total = total.reshape(half, 16, LANES) - own_b[c, :, at] - r_y[c, :, at].astype(f32)
+            wide[c, core, :, pl.ds(pl.multiple_of(tile0 + 16 * g, 16), 16)] = total.astype(bf16)
+
+        @pl.when(has_bwd)
+        def _():
+            copy_g[c].start()
+
+        copy_d[c].start()
+
+    @pl.loop(0, SLAB // 16)
+    def _(g):
+        at = pl.ds(pl.multiple_of(16 * g, 16), 16)
+        cells = jnp.concatenate(
+            [blur[c, :, :, at].reshape(lead, LANES) for c in range(2)], axis=1
+        )
+        resid = mm(kb[...], cells) - observed(at, slice(None)).astype(f32)
+        hs[:, at] = resid.astype(bf16).reshape(bands, 16, 2 * LANES)
 
     stores.append(pltpu.make_async_copy(hs, hs_hbm, out_sem.at[8]))
     stores[0].start()
-
-    for c in range(2):
-        copy_b[c].wait_recv()
-        total = own_b[c] + r_b[c].astype(f32)
-        own_b[c] = total
-        s_y[c, 0] = own_b[c, :, pl.ds(part0, 32)].astype(bf16)
-        copy_y0[c].start()
-        s_y[c, 1] = own_b[c, :, pl.ds(part1, 32)].astype(bf16)
-        copy_y1[c].start()
-
-    for c in range(2):
-        copy_y0[c].wait_recv()
-        wide[c, core, :, pl.ds(far, 32)] = (
-            own_b[c, :, pl.ds(part1, 32)] + r_y[c, 0].astype(f32)
-        ).astype(bf16)
-
-        @pl.when(has_bwd)
-        def _():
-            copy_g[c].start()
-
-        copy_y1[c].wait_recv()
-        wide[c, core, :, 32:64] = (own_b[c, :, pl.ds(part0, 32)] + r_y[c, 1].astype(f32)).astype(bf16)
-        copy_d[c].start()
 
     for c in range(2):
 
@@ -378,7 +410,7 @@
     finish(other, 1 - core, 1)
 
     for c in range(2):
-        for copies in (copy_a, copy_x0, copy_x1, copy_b, copy_y0, copy_y1, copy_d, copy_e):
+        for copies in (copy_a, copy_x0, copy_x1, copy_b, copy_y, copy_d, copy_e):
             copies[c].wait_send()
 
         @pl.when(has_fwd)
@@ -428,11 +460,11 @@
             buf(latent.shape),
             buf(hyper_obs.shape),
             buf(latent.shape, f32),
-            buf((8, LANES)),
             buf((bands, lead)),
             buf((lead, bands)),
             buf((LANES, lead)),
             buf((lead, LANES)),
+            buf((2, lead, lead)),
             buf((2, half, WINDOW, LANES)),
             buf((2, half, WINDOW, LANES)),
             buf((2, half, WINDOW, LANES), f32),
@@ -444,13 +476,13 @@
             buf((2, half, coarse, LANES)),
             buf((2, half, coarse, LANES)),
             buf((2, half, coarse, LANES), f32),
-            buf((2, 2, half, 32, LANES)),
-            buf((2, 2, half, 32, LANES)),
+            buf((2, half, coarse, LANES)),
+            buf((2, half, coarse, LANES)),
             buf((2, 2, half, WINDOW, LANES)),
             pltpu.SemaphoreType.DMA((4,)),
             pltpu.SemaphoreType.DMA((9,)),
-            pltpu.SemaphoreType.DMA((11, 2)),
-            pltpu.SemaphoreType.DMA((11, 2)),
+            pltpu.SemaphoreType.DMA((10, 2)),
+            pltpu.SemaphoreType.DMA((10, 2)),
         ],
         compiler_params=pltpu.CompilerParams(
             collective_id=0, has_side_effects=True, vmem_limit_bytes=56 * 1024 * 1024
@@ -463,8 +495,8 @@
         latent,
         multi_obs,
         hyper_obs,
-        basis,
-        jnp.repeat(response, 16, axis=0),
+        basis.T,
+        response,
         jnp.asarray(cols),
         jnp.asarray(cols.T),
         jnp.asarray(row),

time: 61 us -> 51.4 us (0.84)
  Pallas kernels: 50.8 us -> 44.3 us
  local copies, waits for them, and re-layouts: 9.04 us -> 6.28 us
    pallas_call x1, Pallas kernels: 50.8 us -> 44.3 us  [shards_joined(): pl.pallas_call(joined, out_shape=(jax.ShapeDtypeStruct(latent.shape, bf16...]
    unnamed x5 -> x4, local copies, waits for them, and re-layouts: 7.72 us -> 6.28 us
    broadcast_in_dim x1 -> x0, local copies, waits for them, and re-layouts: 1.32 us -> none  [shards_joined(): jnp.repeat(response, 16, axis=0)]
where the time goes in v3:
time: 51.4 us; the launch traced here: 51.2 us
  Pallas kernels  44.3 us (86%)
  local copies, waits for them, and re-layouts  6.28 us (12%)
  between operations  0.65 us (1%)
    pallas_call x1, Pallas kernels, shards_joined(): pl.pallas_call(joined, out_shape=(jax.ShapeDtypeStruct(latent.shape, bf16...  44.3 us
    unnamed x4, local copies, waits for them, and re-layouts  6.28 us

profile of v3, /device:TPU:8, one launch (start us, length us, event | category | flops | bytes accessed | tf_op | source)
XLA Modules:
  0.0 51.2 jit_solution(10463365832194779077)
XLA Ops:
  0.6 44.3 %joined.1 = (bf16[32,64,1024]{2,1,0:T(8,128)(2,1)}, bf16[56,64,256]{2,1,0:T(8,128)(2,1)}) custom-call(bf16[32,64,1024]{2,1,0:T(8,128)(2,1)} %lat_hbm.1, bf16[8,64,1024]{2,1,0:T(8,128)(2,1)} %mo_hbm.1, bf16[56,64,256]{2,1,0:T(8,128)(2,1)} %hy_hbm.1, bf16[32,224]{1,0:T(8,128)(2,1)} %bitcast.1, bf16[8,224]{1,0:T(8,128)(2,1)} %response.1, ...), custom_call_target="tpu_custom_call" | custom-call | flops 10737418240 | bytes 13631488 | tf_op jit(solution)/shard_map/joined/pallas_call | solution.py:448
  44.9 0.0 copy-start
  44.9 5.0 %copy.13 = bf16[32,64,1024]{2,1,0:T(8,128)(2,1)} copy(bf16[32,64,1024]{2,1,0:T(8,128)(2,1)} %get-tuple-element.4) | data formatting | bytes 8388608
  50.0 0.0 copy-done
  50.0 1.2 %copy.14 = bf16[56,64,256]{2,1,0:T(8,128)(2,1)} copy(bf16[56,64,256]{2,1,0:T(8,128)(2,1)S(1)} %copy-done) | data formatting | bytes 3670016
Async XLA Ops:
  44.9 5.1 %copy-start = (bf16[56,64,256]{2,1,0:T(8,128)(2,1)S(1)}, bf16[56,64,256]{2,1,0:T(8,128)(2,1)}, u32[]{:S(2)}) copy-start(bf16[56,64,256]{2,1,0:T(8,128)(2,1)} %get-tuple-element.5) | copy-start | bytes 5505028

commit v4 on v3

--- a/solution.py
+++ b/solution.py
@@ -122,9 +122,9 @@
 
 
 def joined(
-    lat_hbm, mo_hbm, hy_hbm, basis_t, response, kc, kct, kri, krt,
-    z_hbm, hs_hbm,
-    lat, mo, hy, z, hs, base, kb, kbt, km, kmt, ks,
+    lat_hbm, mo_hbm, hy_hbm, basis_t, response, kc, kri, krt,
+    sp_hbm, ms_hbm, kmt_hbm, hs_hbm,
+    lat, mo, hy, sp, hs, msr, kb, kbt, km, kmt, ks,
     s_a, r_a, own, s_h, r_h, s_x, r_x, blur, s_b, r_b, own_b, s_y, r_y, wide,
     in_sem, out_sem, send_sem, recv_sem,
 ):
@@ -290,13 +290,10 @@
         copy_x0[c].start()
         own[c, :, pl.ds(far, 32)] = own[c, :, pl.ds(far, 32)] + r_a[c, :, pl.ds(far, 32)].astype(f32)
 
-    pick = same((bands * 16, all_bands), lambda i: (i >> 4) + bands * s, plain).astype(bf16)
     repeated = jnp.broadcast_to(
         response[...].astype(f32)[:, None, :], (response.shape[0], 16, all_bands)
     )
     repeated = repeated.reshape(LANES, all_bands).astype(bf16)
-    picked = mm_nt(pick, basis_t[...]).astype(bf16)
-    kb[...] = (mm(picked, spread_q) * same((bands * 16, lead), low, low)).astype(bf16)
     mixed = mm_nt(repeated, basis_t[...]).astype(bf16)
     km[...] = (mm(mixed, spread_q) * same((LANES, lead), low, low)).astype(bf16)
     kmt[...] = (mm_nt(tall, repeated) * same((lead, LANES), low, low)).astype(bf16)
@@ -318,6 +315,9 @@
         copy_x1[c].start()
 
     share(1)
+    pick = same((bands * 16, all_bands), lambda i: (i >> 4) + bands * s, plain).astype(bf16)
+    picked = mm_nt(pick, basis_t[...]).astype(bf16)
+    kb[...] = (mm(picked, spread_q) * same((bands * 16, lead), low, low)).astype(bf16)
     loads[2].wait()
 
     @pl.loop(0, SLAB // 16)
@@ -327,8 +327,7 @@
             cut = slice(256 * n, 256 * n + 256)
             cells = lat[:, at, cut].reshape(lead, 256)
             resid = mm(km[...], cells) - mo[:, at, cut].reshape(LANES, 256).astype(f32)
-            back = mm(kmt[...], resid.astype(bf16))
-            base[:, at, cut] = (cells.astype(f32) - STEP * back).reshape(-1, 16, 256)
+            msr[:, at, cut] = resid.astype(bf16).reshape(-1, 16, 256)
 
     for c in range(2):
         copy_x0[c].wait_recv()
@@ -339,7 +338,12 @@
         blur[c, core, :, pl.ds(part0, 32)] = (own[c, :, 32:64] + r_x[c, 1].astype(f32)).astype(bf16)
         copy_c[c].start()
 
-    stores = []
+    stores = [
+        pltpu.make_async_copy(msr, ms_hbm, out_sem.at[0]),
+        pltpu.make_async_copy(kmt, kmt_hbm, out_sem.at[1]),
+    ]
+    for store in stores:
+        store.start()
     for c in range(2):
         copy_c[c].wait()
         copy_y[c].wait_recv()
@@ -368,8 +372,8 @@
         resid = mm(kb[...], cells) - observed(at, slice(None)).astype(f32)
         hs[:, at] = resid.astype(bf16).reshape(bands, 16, 2 * LANES)
 
-    stores.append(pltpu.make_async_copy(hs, hs_hbm, out_sem.at[8]))
-    stores[0].start()
+    stores.append(pltpu.make_async_copy(hs, hs_hbm, out_sem.at[2]))
+    stores[2].start()
 
     for c in range(2):
 
@@ -389,25 +393,21 @@
                 [wide[c, who, pl.ds(4 * g, 4)].reshape(4 * WINDOW, LANES) for c in range(2)], axis=1
             )
             rows = mm(krt[core], cells).astype(bf16)
-            at = pl.ds(first + 4 * g, 4)
-            for n in range(lat.shape[2] // 256):
-                cut = slice(256 * n, 256 * n + 256)
-                back = mm(rows, kct[:, cut]).reshape(4, SLAB, 256)
-                z[at, :, cut] = (base[at, :, cut] - STEP * back).astype(bf16)
+            sp[pl.ds(first + 4 * g, 4)] = rows.reshape(4, SLAB, 2 * LANES)
             return carry
 
         lax.fori_loop(0, half // 4, group, 0)
         store = pltpu.make_async_copy(
-            z.at[pl.ds(first, half)], z_hbm.at[pl.ds(first, half)], out_sem.at[slot]
+            sp.at[pl.ds(first, half)], sp_hbm.at[pl.ds(first, half)], out_sem.at[slot]
         )
         store.start()
         stores.append(store)
 
-    finish(mine, core, 0)
+    finish(mine, core, 3)
     for c in range(2):
         copy_d[c].wait_recv()
         copy_e[c].wait_recv()
-    finish(other, 1 - core, 1)
+    finish(other, 1 - core, 4)
 
     for c in range(2):
         for copies in (copy_a, copy_x0, copy_x1, copy_b, copy_y, copy_d, copy_e):
@@ -423,6 +423,26 @@
 
     for store in stores:
         store.wait()
+
+
+def update(lat, sp, msr, kmt, kct, hs_from, z, hs_to, sem):
+    passed = pltpu.make_async_copy(hs_from, hs_to, sem)
+
+    @pl.when(pl.program_id(0) == 0)
+    def _():
+        passed.start()
+
+    lead = lat.shape[0] * 16
+    near = sp[...].reshape(lead, sp.shape[2])
+    for n in range(lat.shape[2] // 256):
+        cut = slice(256 * n, 256 * n + 256)
+        back = mm(near, kct[:, cut]) + mm(kmt[...], msr[:, :, cut].reshape(LANES, 256))
+        cells = lat[:, :, cut].reshape(lead, 256).astype(f32)
+        z[:, :, cut] = (cells - STEP * back).astype(bf16).reshape(-1, 16, 256)
+
+    @pl.when(pl.program_id(0) == pl.num_programs(0) - 1)
+    def _():
+        passed.wait()
 
 
 def row_window(core):
@@ -445,21 +465,23 @@
 
     any_spec = pl.BlockSpec(memory_space=pl.ANY)
     vmem_spec = pl.BlockSpec(memory_space=pltpu.VMEM)
-    return pl.pallas_call(
+    spread, multi_resid, mix, residual = pl.pallas_call(
         joined,
         out_shape=(
-            jax.ShapeDtypeStruct(latent.shape, bf16),
+            jax.ShapeDtypeStruct(latent.shape[:2] + (low_cols,), bf16),
+            jax.ShapeDtypeStruct(multi_obs.shape, bf16),
+            jax.ShapeDtypeStruct((lead, LANES), bf16),
             jax.ShapeDtypeStruct(hyper_obs.shape, bf16),
         ),
-        in_specs=[any_spec] * 3 + [vmem_spec] * 6,
-        out_specs=(any_spec, any_spec),
+        in_specs=[any_spec] * 3 + [vmem_spec] * 5,
+        out_specs=(any_spec,) * 4,
         scratch_shapes=[
             buf(latent.shape),
             buf(multi_obs.shape),
             buf(hyper_obs.shape),
-            buf(latent.shape),
+            buf(latent.shape[:2] + (low_cols,)),
             buf(hyper_obs.shape),
-            buf(latent.shape, f32),
+            buf(multi_obs.shape),
             buf((bands, lead)),
             buf((lead, bands)),
             buf((LANES, lead)),
@@ -480,7 +502,7 @@
             buf((2, half, coarse, LANES)),
             buf((2, 2, half, WINDOW, LANES)),
             pltpu.SemaphoreType.DMA((4,)),
-            pltpu.SemaphoreType.DMA((9,)),
+            pltpu.SemaphoreType.DMA((5,)),
             pltpu.SemaphoreType.DMA((10, 2)),
             pltpu.SemaphoreType.DMA((10, 2)),
         ],
@@ -498,10 +520,34 @@
         basis.T,
         response,
         jnp.asarray(cols),
-        jnp.asarray(cols.T),
         jnp.asarray(row),
         jnp.asarray(row.transpose(0, 2, 1)),
     )
+    rows = 16
+    full = latent.shape[2]
+    return pl.pallas_call(
+        update,
+        grid=(latent.shape[1] // rows,),
+        out_shape=(
+            jax.ShapeDtypeStruct(latent.shape, bf16),
+            jax.ShapeDtypeStruct(hyper_obs.shape, bf16),
+        ),
+        in_specs=[
+            pl.BlockSpec((latent.shape[0], rows, full), lambda g: (0, g, 0)),
+            pl.BlockSpec((latent.shape[0], rows, low_cols), lambda g: (0, g, 0)),
+            pl.BlockSpec((multi_obs.shape[0], rows, full), lambda g: (0, g, 0)),
+            pl.BlockSpec((lead, LANES), lambda g: (0, 0)),
+            pl.BlockSpec((low_cols, full), lambda g: (0, 0)),
+            any_spec,
+        ],
+        out_specs=(
+            pl.BlockSpec((latent.shape[0], rows, full), lambda g: (0, g, 0)),
+            any_spec,
+        ),
+        scratch_shapes=[pltpu.SemaphoreType.DMA(())],
+        compiler_params=pltpu.CompilerParams(vmem_limit_bytes=32 * 1024 * 1024),
+        name="update",
+    )(latent, spread, multi_resid, mix, jnp.asarray(cols.T), residual)
 
 
 def shards(latent, basis, response, hyper_obs, multi_obs):

time: 51.4 us -> 52.2 us (1.016); the launches traced: 51.2 us -> 51.3 us
  Pallas kernels: 44.3 us -> 45.8 us
  local copies, waits for them, and re-layouts: 6.28 us -> 4.86 us
    pallas_call x1 -> x2, Pallas kernels: 44.3 us -> 45.8 us  [the longest x1 41.4 us: shards_joined(): pl.pallas_call(joined, out_shape=(jax.ShapeDtypeStruct(latent.shape[:2] +...]
    unnamed x4 -> x12, local copies, waits for them, and re-layouts: 6.28 us -> 4.86 us
where the time goes in v4:
time: 52.2 us; the launch traced here: 51.3 us
  Pallas kernels  45.8 us (88%)
  local copies, waits for them, and re-layouts  4.86 us (9%)
  between operations  0.68 us (1%)
    pallas_call x1, Pallas kernels, shards_joined(): pl.pallas_call(joined, out_shape=(jax.ShapeDtypeStruct(latent.shape[:2] +...  41.4 us
    unnamed x12, local copies, waits for them, and re-layouts  4.86 us
    pallas_call x1, Pallas kernels, shards_joined(): pl.pallas_call(update, grid=(latent.shape[1] // rows,), out_shape=(jax.Sh...  4.4 us

profile of v4, /device:TPU:8, one launch (start us, length us, event | category | flops | bytes accessed | tf_op | source)
XLA Modules:
  0.0 51.3 jit_solution(5810916573937471399)
XLA Ops:
  0.6 0.0 copy-start
  0.6 0.0 copy-start.4
  0.7 41.4 %joined.1 = (bf16[32,64,256]{2,1,0:T(8,128)(2,1)}, bf16[8,64,1024]{2,1,0:T(8,128)(2,1)}, bf16[512,128]{1,0:T(8,128)(2,1)}, bf16[56,64,256]{2,1,0:T(8,128)(2,1)}) custom-call(bf16[32,64,1024]{2,1,0:T(8,128)(2,1)} %lat.1, bf16[8,64,1024]{2,1,0:T(8,128)(2,1)} %mo_hbm.1, bf16[56,64,256]{2,1,0:T(8,128)(2,1)} %hy_hbm.1, bf16[32,224]{1,0:T(8,128)(2,1)} %bitcast.1, ...), custom_call_target="tpu_custom_call" | custom-call | flops 10737418240 | bytes 13631488 | tf_op jit(solution)/shard_map/joined/pallas_call | solution.py:468
  42.0 0.0 copy-done
  42.0 0.0 copy-done.4
  42.0 0.0 copy-start.1
  42.0 1.5 %copy-done.1 = bf16[56,64,256]{2,1,0:T(8,128)(2,1)S(1)} copy-done((bf16[56,64,256]{2,1,0:T(8,128)(2,1)S(1)}, bf16[56,64,256]{2,1,0:T(8,128)(2,1)}, u32[]{:S(2)}) %copy-start.1) | copy-done | bytes 1835032
  43.5 0.0 copy-start.2
  43.5 1.2 %copy-done.2 = bf16[32,64,256]{2,1,0:T(8,128)(2,1)S(1)} copy-done((bf16[32,64,256]{2,1,0:T(8,128)(2,1)S(1)}, bf16[32,64,256]{2,1,0:T(8,128)(2,1)}, u32[]{:S(2)}) %copy-start.2) | copy-done | bytes 1048600
  44.8 0.0 copy-start.3
  44.8 1.2 %copy-done.3 = bf16[8,64,1024]{2,1,0:T(8,128)(2,1)S(1)} copy-done((bf16[8,64,1024]{2,1,0:T(8,128)(2,1)S(1)}, bf16[8,64,1024]{2,1,0:T(8,128)(2,1)}, u32[]{:S(2)}) %copy-start.3) | copy-done | bytes 1048600
  46.0 0.0 copy-start.5
  46.0 0.9 %copy-done.5 = bf16[512,128]{1,0:T(8,128)(2,1)S(1)} copy-done((bf16[512,128]{1,0:T(8,128)(2,1)S(1)}, bf16[512,128]{1,0:T(8,128)(2,1)}, u32[]{:S(2)}) %copy-start.5) | copy-done | bytes 131096
  46.9 4.4 %update.1 = (bf16[32,64,1024]{2,1,0:T(8,128)(2,1)}, bf16[56,64,256]{2,1,0:T(8,128)(2,1)}) custom-call(bf16[32,64,1024]{2,1,0:T(8,128)(2,1)S(1)} %copy-done, bf16[32,64,256]{2,1,0:T(8,128)(2,1)S(1)} %copy-done.2, bf16[8,64,1024]{2,1,0:T(8,128)(2,1)S(1)} %copy-done.3, bf16[512,128]{1,0:T(8,128)(2,1)S(1)} %copy-done.5, bf16[256,1024]{1,0:T(8,128)(2,1)S(1)} %copy-done.4, ...), custom_call_target="tpu_custom_call" | custom-call | tf_op jit(solution)/shard_map/update/pallas_call | solution.py:528
Async XLA Ops:
  0.6 41.4 %copy-start = (bf16[32,64,1024]{2,1,0:T(8,128)(2,1)S(1)}, bf16[32,64,1024]{2,1,0:T(8,128)(2,1)}, u32[]{:S(2)}) copy-start(bf16[32,64,1024]{2,1,0:T(8,128)(2,1)} %lat.1) | copy-start | bytes 12582916
  0.6 41.4 %copy-start.4 = (bf16[256,1024]{1,0:T(8,128)(2,1)S(1)}, bf16[256,1024]{1,0:T(8,128)(2,1)}, u32[]{:S(2)}) copy-start(bf16[256,1024]{1,0:T(8,128)(2,1)} %constant.11.clone.kct) | copy-start | bytes 1572868
  42.0 1.5 %copy-start.1 = (bf16[56,64,256]{2,1,0:T(8,128)(2,1)S(1)}, bf16[56,64,256]{2,1,0:T(8,128)(2,1)}, u32[]{:S(2)}) copy-start(bf16[56,64,256]{2,1,0:T(8,128)(2,1)} %get-tuple-element.9.hs_from) | copy-start | bytes 5505028
  43.5 1.2 %copy-start.2 = (bf16[32,64,256]{2,1,0:T(8,128)(2,1)S(1)}, bf16[32,64,256]{2,1,0:T(8,128)(2,1)}, u32[]{:S(2)}) copy-start(bf16[32,64,256]{2,1,0:T(8,128)(2,1)} %get-tuple-element.6.sp) | copy-start | bytes 3145732
  44.8 1.2 %copy-start.3 = (bf16[8,64,1024]{2,1,0:T(8,128)(2,1)S(1)}, bf16[8,64,1024]{2,1,0:T(8,128)(2,1)}, u32[]{:S(2)}) copy-start(bf16[8,64,1024]{2,1,0:T(8,128)(2,1)} %get-tuple-element.7.msr) | copy-start | bytes 3145732
  46.0 0.9 %copy-start.5 = (bf16[512,128]{1,0:T(8,128)(2,1)S(1)}, bf16[512,128]{1,0:T(8,128)(2,1)}, u32[]{:S(2)}) copy-start(bf16[512,128]{1,0:T(8,128)(2,1)} %get-tuple-element.8.kmt) | copy-start | bytes 393220

commit v5 on v4

--- a/solution.py
+++ b/solution.py
@@ -545,7 +545,7 @@
             any_spec,
         ),
         scratch_shapes=[pltpu.SemaphoreType.DMA(())],
-        compiler_params=pltpu.CompilerParams(vmem_limit_bytes=32 * 1024 * 1024),
+        compiler_params=pltpu.CompilerParams(vmem_limit_bytes=62 * 1024 * 1024),
         name="update",
     )(latent, spread, multi_resid, mix, jnp.asarray(cols.T), residual)
 

time: 52.2 us -> 102 us (1.95)
  Pallas kernels: 45.8 us -> 100 us
  local copies, waits for them, and re-layouts: 4.86 us -> 0 us
    pallas_call x1, Pallas kernels: 4.4 us -> 59.2 us  [shards_joined(): pl.pallas_call(update, grid=(latent.shape[1] // rows,), out_shape=(jax.Sh...]
    unnamed x12 -> x0, local copies, waits for them, and re-layouts: 4.86 us -> none
where the time goes in v5:
time: 102 us; the launch traced here: 101 us
  Pallas kernels  100 us (98%)
    pallas_call x1, Pallas kernels, shards_joined(): pl.pallas_call(update, grid=(latent.shape[1] // rows,), out_shape=(jax.Sh...  59.2 us
    pallas_call x1, Pallas kernels, shards_joined(): pl.pallas_call(joined, out_shape=(jax.ShapeDtypeStruct(latent.shape[:2] +...  40.9 us

profile of v5, /device:TPU:8, one launch (start us, length us, event | category | flops | bytes accessed | tf_op | source)
XLA Modules:
  0.0 100.7 jit_solution(7940947406786793574)
XLA Ops:
  0.6 40.9 %joined.1 = (bf16[32,64,256]{2,1,0:T(8,128)(2,1)}, bf16[8,64,1024]{2,1,0:T(8,128)(2,1)}, bf16[512,128]{1,0:T(8,128)(2,1)}, bf16[56,64,256]{2,1,0:T(8,128)(2,1)}) custom-call(bf16[32,64,1024]{2,1,0:T(8,128)(2,1)} %lat.1, bf16[8,64,1024]{2,1,0:T(8,128)(2,1)} %mo_hbm.1, bf16[56,64,256]{2,1,0:T(8,128)(2,1)} %hy_hbm.1, bf16[32,224]{1,0:T(8,128)(2,1)} %bitcast.1, ...), custom_call_target="tpu_custom_call" | custom-call | flops 10737418240 | bytes 13631488 | tf_op jit(solution)/shard_map/joined/pallas_call | solution.py:468
  41.5 59.2 %update.1 = (bf16[32,64,1024]{2,1,0:T(8,128)(2,1)}, bf16[56,64,256]{2,1,0:T(8,128)(2,1)}) custom-call(bf16[32,64,1024]{2,1,0:T(8,128)(2,1)} %lat.1, bf16[32,64,256]{2,1,0:T(8,128)(2,1)} %get-tuple-element.6.sp, bf16[8,64,1024]{2,1,0:T(8,128)(2,1)} %get-tuple-element.7.msr, bf16[512,128]{1,0:T(8,128)(2,1)} %get-tuple-element.8.kmt, ...), custom_call_target="tpu_custom_call" | custom-call | tf_op jit(solution)/shard_map/update/pallas_call | solution.py:528
